TPU v7x, 128 devices: a whole 4x4x4 slice. The times are simulated.
128 devices in a mesh: wide: 8 (over x, core), sixteen: 16 (over y, z).
Axes of the slice: x: 4, y: 4, z: 4, core: 2. Of those that a mesh axis runs over, the one named last changes fastest.
Arguments:
- features: float32 [8, 16, 512, 128], P('wide', 'sixteen'), may hold values from -6 to 6
- positions: float32 [8, 16, 3, 512], P('wide', 'sixteen'), may hold values from 0 to 1, as said below
- tile_lists: int32 [8, 16, 4, 16], P('wide', 'sixteen'), may hold values from 0 to 36, as said below
- value_proj: float32 [128, 128], replicated, may hold values from -0.5 to 0.5
- radial_mix: float32 [16, 128], replicated, may hold values from -1.5 to 1.5
- charge_proj: float32 [128, 128], replicated, may hold values from -0.5 to 0.5
- screening: float32 [128], P(('wide', 'sixteen')), may hold values from 20 to 200
- smearing: float32 [128], P(('wide', 'sixteen')), may hold values from 0.003 to 0.02
- mesh_gain: float32 [128], replicated, may hold values from 0.25 to 1.75
- mesh_up: float32 [128, 256], replicated, may hold values from -0.5 to 0.5
- mesh_down: float32 [256, 128], replicated, may hold values from -0.375 to 0.375
- long_proj: float32 [128, 128], replicated, may hold values from -0.5 to 0.5
- atom_gain: float32 [128], replicated, may hold values from 0.25 to 1.75
- atom_up: float32 [128, 256], replicated, may hold values from -0.5 to 0.5
- atom_down: float32 [256, 128], replicated, may hold values from -0.375 to 0.375
Outputs:
- updated: float32 [8, 16, 512, 128], P('wide', 'sixteen')
Inputs may be any that keep to these rules, and one draw needn't show every extreme that they name: `tile_lists`: each list of tile t of a block holds codes nb * 4 + t2 of tiles of the 3 x 3 blocks around it with (t2 - t) mod 4 equal to 0, 1 or 3; its first entry is the tile itself, 16 + t; its live entries are distinct; empty entries hold 36 and stand after all live ones; every list has 1 to 16 live entries and some list has 16. `positions`: the third coordinate of atom a of a block lies between a / 512 and (a + 1) / 512.
All inputs are finite; a program needn't handle non-finite values.
Results may differ from a plain program's by a relative error of at most 0.0003.
Values sent between devices are 32-bit elements; how exact they have to be, the bound alone decides.
No kernel may reach another device: no remote copies, remote signals or barrier semaphores. Data moves between devices by JAX's collectives and lax.ppermute only.
A program may use at most 64 MiB of HBM per device.

v0:
```python
import functools
import math

import jax
import jax.numpy as jnp
import ml_dtypes
import numpy as np
from jax import lax
from jax.experimental import pallas as pl
from jax.experimental.pallas import tpu as pltpu
from jax.sharding import PartitionSpec as P

F32 = jnp.float32
BF = jnp.bfloat16
MESH = 64
LANES = 128
ATOMS = 512
CHUNK = 64
CHUNKS = ATOMS // CHUNK
BASES = 16
ROWS = 24
PACK = 528
FAR = 1000.0
CUTOFF = 0.05
MID = 8
LIMIT = 48 * 1024 * 1024


def split(x):
    hi = x.astype(BF)
    return hi, (x - hi.astype(F32)).astype(BF)


def dot(a, b):
    return jnp.dot(a, b, preferred_element_type=F32)


def dot_nt(a, b):
    return lax.dot_general(a, b, (((1,), (1,)), ((), ())), preferred_element_type=F32)


def dot3(a, b):
    ah, al = split(a)
    bh, bl = split(b)
    return dot(ah, bh) + (dot(ah, bl) + dot(al, bh))


def lane_iota(shape):
    return lax.broadcasted_iota(jnp.int32, shape, len(shape) - 1)


def half_turn(x):
    return pltpu.roll(x, 64, x.ndim - 1)


def pack_body(feat_ref, pos_ref, proj_ref, out_ref):
    out_ref[0:ATOMS, :] = dot3(feat_ref[...], proj_ref[...])
    for d in range(3):
        for t in range(4):
            row = ATOMS + 4 * d + t
            out_ref[row : row + 1, :] = pos_ref[d : d + 1, t * LANES : (t + 1) * LANES]
    out_ref[ATOMS + 12 : PACK, :] = jnp.zeros((PACK - ATOMS - 12, LANES), F32)


class Hats:
    def __init__(self, pos):
        filled = jnp.concatenate([pos, jnp.zeros((5, ATOMS), F32)], axis=0)
        columns = filled.T
        wide = lambda d, scale: jnp.broadcast_to(columns[:, d : d + 1] * scale, (ATOMS, LANES))
        self.ux = wide(0, 8.0)
        self.uy = wide(1, 4.0)
        lane = lane_iota((1, LANES))
        self.half = (lane // 64).astype(F32)
        self.low = lane < 64
        depth = jnp.abs(wide(2, float(MESH)) - (lane % 64).astype(F32))
        self.hz = jnp.maximum(1.0 - jnp.minimum(depth, 64.0 - depth), 0.0)
        self.pairs = [self.y(2.0 * h + self.half) * self.hz for h in range(2)]
        self.top = self.y(4.0) * self.hz

    def x(self, cell):
        return jnp.maximum(1.0 - jnp.abs(self.ux - cell), 0.0)

    def y(self, cell):
        return jnp.maximum(1.0 - jnp.abs(self.uy - cell), 0.0)

    def row(self, r):
        if r < 16:
            return self.x(float(r % 8)) * self.pairs[r // 8]
        x = r - 16
        low = self.x(float(x)) * self.top
        if x < 4:
            high = self.x(8.0) * (self.y(float(x)) * self.hz)
        elif x == 4:
            high = self.x(8.0) * self.top
        else:
            high = 0.0
        return jnp.where(self.low, low, high)

    def two_rows(self, r):
        return split(jnp.concatenate([self.row(r), self.row(r + 1)], axis=1))


def spread_body(feat_ref, pos_ref, proj_ref, out_ref):
    charges = dot3(feat_ref[...], proj_ref[...])
    high, low = split(charges.T)
    both = jnp.concatenate([high, low], axis=0)
    hats = Hats(pos_ref[...])
    for r in range(0, ROWS, 2):
        wh, wl = hats.two_rows(r)
        first = dot(both, wh)
        result = (first[:LANES] + first[LANES:]) + dot(high, wl)
        for k in range(2):
            out_ref[pl.ds(r + k, LANES, stride=ROWS), :] = result[:, k * LANES : (k + 1) * LANES]


def real_basis():
    n = np.arange(MESH)
    rows = []
    for k in range(MESH):
        if k == 0:
            rows.append(np.full(MESH, 1.0 / 8.0))
        elif k == MESH // 2:
            rows.append(np.where(n % 2 == 0, 1.0, -1.0) / 8.0)
        elif k < MESH // 2:
            rows.append(np.cos(2 * np.pi * (k * n % MESH) / MESH) * math.sqrt(2.0) / 8.0)
        else:
            rows.append(np.sin(2 * np.pi * ((MESH - k) * n % MESH) / MESH) * math.sqrt(2.0) / 8.0)
    return np.stack(rows)


def halves(table):
    high = table.astype(np.float32).astype(ml_dtypes.bfloat16)
    low = (table - high.astype(np.float64)).astype(np.float32).astype(ml_dtypes.bfloat16)
    return high, low


def stacked(table):
    high, low = halves(table)
    return np.concatenate([high, low, high], axis=1)


def squared(table):
    high, low = halves(table)
    top = np.concatenate([high, low], axis=1)
    bottom = np.concatenate([high, np.zeros_like(low)], axis=1)
    return np.concatenate([top, bottom], axis=0)


def filter_tables():
    q = real_basis()
    y_forward = np.concatenate([q[:, 0::2], q[:, 1::2]], axis=0)
    y_back = np.concatenate([q.T[0::2], q.T[1::2]], axis=0)
    twice = np.kron(np.eye(2), q.T)
    return (
        stacked(q),
        stacked(y_forward),
        squared(twice),
        squared(twice.T),
        stacked(y_back),
        stacked(q.T),
    )


def stack_rows(x):
    high, low = split(x)
    return jnp.concatenate([high, high, low], axis=0)


def sum_halves(x):
    return x[:, :LANES] + x[:, LANES:]


def filter_body(
    screen_ref, smear_ref, in_ref, xf_ref, yf_ref, zf_ref, zb_ref, yb_ref, xb_ref, out_ref, turn_ref, edge_ref
):
    devices = 128
    low = lane_iota((1, LANES)) < 64
    place = lax.broadcasted_iota(jnp.int32, (devices, 1), 0) % 16

    side = [in_ref[pl.ds(16 + y, devices, stride=ROWS), :] for y in range(5)]
    corner = jnp.where(place == 0, pltpu.roll(side[4], 113, 0), pltpu.roll(side[4], 1, 0))
    side[0] = side[0] + corner
    for h in range(2):
        both = jnp.where(low, half_turn(side[2 * h]), side[2 * h + 1])
        edge_ref[h * devices : (h + 1) * devices, :] = pltpu.roll(both, 16, 0)

    first_row = lax.broadcasted_iota(jnp.int32, (8, 1), 0) == 0
    x_forward = xf_ref[...]
    for s in range(16):
        parts = []
        for h in range(2):
            tiles = []
            for w in range(8):
                at = w * 16 + s
                tile = in_ref[at * ROWS + h * 8 : at * ROWS + h * 8 + 8, :]
                edge = edge_ref[h * devices + at : h * devices + at + 1, :]
                tile = tile + jnp.where(first_row, edge, 0.0)
                if h == 0:
                    below = (w * 16 + (s + 15) % 16) * ROWS + 16
                    tile = tile + jnp.where(low, in_ref[below : below + 8, :], 0.0)
                tiles.append(tile)
            parts.append(jnp.concatenate(tiles, axis=0))
        result = dot(x_forward, stack_rows(jnp.concatenate(parts, axis=1)))
        for h in range(2):
            turn_ref[pl.ds(2 * s + h, MESH, stride=32), :] = result[:, h * LANES : (h + 1) * LANES]

    kappa = screen_ref[0]
    kappa_sq = kappa * kappa
    decay = -0.5 * smear_ref[0] * smear_ref[0]
    lane = lane_iota((1, LANES))
    fold = lambda k: jnp.minimum(k, MESH - k).astype(F32)
    nz = fold(lane % 64)
    ny = fold(lax.broadcasted_iota(jnp.int32, (MESH, 1), 0))
    scale = 4.0 * math.pi**2
    yz = (ny * ny + nz * nz) * scale
    y_forward, z_forward = yf_ref[...], zf_ref[...]
    z_back, y_back = zb_ref[...], yb_ref[...]
    group = 4
    for start in range(0, 32, group):
        planes = []
        for p in range(start, start + group):
            pair = jnp.concatenate(
                [turn_ref[(2 * p + k) * 32 : (2 * p + k + 1) * 32, :] for k in range(2)], axis=1
            )
            result = dot(y_forward, stack_rows(pair))
            a, b = result[:, :LANES], result[:, LANES:]
            straight = jnp.where(low, a[:MESH], b[MESH:])
            planes.append(straight + half_turn(jnp.where(low, b[:MESH], a[MESH:])))
        stack = jnp.concatenate(planes, axis=0)
        stack = sum_halves(dot(jnp.concatenate(split(stack), axis=1), z_forward))
        gains = []
        for p in range(start, start + group):
            nx = fold(2 * p + lane // 64)
            square = yz + nx * nx * scale
            gains.append(kappa_sq * jnp.exp(square * decay) / (square + kappa_sq))
        stack = stack * jnp.concatenate(gains, axis=0)
        stack = sum_halves(dot(jnp.concatenate(split(stack), axis=1), z_back))
        for g in range(0, group, 2):
            pair = jnp.concatenate([stack[(g + k) * MESH : (g + k + 1) * MESH] for k in range(2)], axis=1)
            result = dot(y_back, stack_rows(pair))
            for k in range(2):
                p = start + g + k
                a = result[:32, k * LANES : (k + 1) * LANES]
                b = result[32:, k * LANES : (k + 1) * LANES]
                turn_ref[2 * p * 32 : 2 * p * 32 + 32, :] = jnp.where(low, a, half_turn(b))
                turn_ref[2 * p * 32 + 32 : 2 * p * 32 + 64, :] = jnp.where(low, half_turn(a), b)

    x_back = xb_ref[...]
    for s in range(16):
        pair = jnp.concatenate(
            [turn_ref[pl.ds(2 * s + h, MESH, stride=32), :] for h in range(2)], axis=1
        )
        result = dot(x_back, stack_rows(pair))
        for w in range(8):
            at = (w * 16 + s) * ROWS
            for h in range(2):
                tile = result[w * 8 : (w + 1) * 8, h * LANES : (h + 1) * LANES]
                out_ref[at + h * 8 : at + h * 8 + 8, :] = tile
                if h == 0:
                    below = (w * 16 + (s + 15) % 16) * ROWS + 16
                    out_ref[below : below + 8, :] = jnp.where(low, tile, 0.0)

    ahead = [pltpu.roll(out_ref[pl.ds(8 * h, devices, stride=ROWS), :], 112, 0) for h in range(2)]
    turned = [half_turn(x) for x in ahead]
    corner = jnp.where(place == 15, pltpu.roll(turned[0], 15, 0), pltpu.roll(turned[0], 127, 0))
    for y, high in enumerate([turned[0], ahead[0], turned[1], ahead[1], corner]):
        rows = pl.ds(16 + y, devices, stride=ROWS)
        out_ref[rows, :] = jnp.where(low, out_ref[rows, :], high)


ENVELOPE = (
    0.9999999991137324,
    -0.4674010362718563,
    0.0945531128786198,
    -0.011119339660821159,
    0.0008600612678157039,
    -4.252312938118321e-05,
)


def short_body(live_ref, near_ref, left_ref, right_ref, mix_ref, out_ref, val_ref, win_ref, own_ref, sum_ref):
    lane = lane_iota((1, LANES))
    pos = near_ref[PACK + ATOMS : PACK + ATOMS + 16, :]
    for d, scale in ((0, 0.125), (1, 0.0625), (2, 1.0)):
        for t in range(4):
            row = pos[4 * d + t : 4 * d + t + 1, :] * scale
            own_ref[d * ATOMS + t * LANES : d * ATOMS + (t + 1) * LANES, :] = jnp.broadcast_to(
                row, (LANES, LANES)
            ).T

    for nb in range(9):
        dx, dy = nb // 3 - 1, nb % 3 - 1
        ref = (left_ref, near_ref, right_ref)[dx + 1]
        base = (dy + 1) * PACK
        high, low = split(ref[base : base + ATOMS, :])
        both = jnp.concatenate([high, low], axis=1)
        val_ref[nb, 32 : 32 + ATOMS, :] = both
        val_ref[nb, 0:32, :] = both[ATOMS - 32 :, :]
        val_ref[nb, ATOMS + 32 :, :] = both[:32, :]
        pos = ref[base + ATOMS : base + PACK, :]
        for m in range(CHUNKS):
            t = m // 2
            turned = pltpu.roll(pos, 32 if m % 2 == 0 else 96, 1)
            first, second = ((t + 3) % 4, t) if m % 2 == 0 else (t, (t + 1) % 4)
            from_first = lane < (32 if m % 2 == 0 else 96)
            for d in range(3):
                a = turned[4 * d + first : 4 * d + first + 1, :]
                b = turned[4 * d + second : 4 * d + second + 1, :]
                if d == 0:
                    row = (jnp.where(from_first, a, b) + float(dx)) * 0.125
                elif d == 1:
                    row = (jnp.where(from_first, a, b) + float(dy)) * 0.0625
                else:
                    if m == 0:
                        a = a - 1.0
                    if m == CHUNKS - 1:
                        b = b + 1.0
                    row = jnp.where(from_first, a, b)
                win_ref[nb, m, d : d + 1, :] = row

    me = lax.broadcasted_iota(jnp.int32, (CHUNK, LANES), 0) + 32
    itself = (me == lane_iota((CHUNK, LANES))).astype(F32)
    zero = jnp.zeros((LANES, LANES), BF)

    def chunk(m, carry):
        t = m // 2
        even = m % 2 == 0
        tile_a = jnp.where(even, (t + 3) % 4, t)
        tile_b = jnp.where(even, t, (t + 1) % 4)
        from_first = lane < jnp.where(even, 32, 96)
        sum_ref[...] = jnp.zeros_like(sum_ref)
        start = pl.multiple_of(m * CHUNK, CHUNK)

        def block(nb, carry):
            live_a = live_ref[t, nb * 4 + tile_a]
            live_b = live_ref[t, nb * 4 + tile_b]

            @pl.when(live_a + live_b > 0)
            def _():
                window = win_ref[nb, m]
                far_a = (1 - live_a).astype(F32) * FAR
                far_b = (1 - live_b).astype(F32) * FAR
                xj = window[0:1] + jnp.where(from_first, far_a, far_b)
                dx = xj - own_ref[pl.ds(start, CHUNK), :]
                dy = window[1:2] - own_ref[pl.ds(ATOMS + start, CHUNK), :]
                dz = window[2:3] - own_ref[pl.ds(2 * ATOMS + start, CHUNK), :]
                s = (dx * dx + dy * dy + dz * dz) * (1.0 / CUTOFF**2)
                s = jnp.maximum(s, itself * jnp.where(nb == 4, 1.0, 0.0))
                s = jnp.minimum(s, 1.0)
                q = s * lax.rsqrt(jnp.maximum(s, 1e-30))
                v = q * float(BASES - 1) - float(MID)
                env = jnp.full_like(s, ENVELOPE[-1])
                for c in ENVELOPE[-2::-1]:
                    env = env * s + c
                rest = 1.0 - s
                middle = jnp.exp(-0.5 * v * v) * (env * (rest * rest))
                up, down = jnp.exp(v), jnp.exp(-v)
                terms = [None] * BASES
                terms[MID] = middle
                for b in range(MID + 1, BASES):
                    terms[b] = terms[b - 1] * up
                for b in range(MID - 1, -1, -1):
                    terms[b] = terms[b + 1] * down
                lhs = jnp.concatenate([jnp.concatenate(split(x), axis=1) for x in terms], axis=0)
                values = val_ref[nb, pl.ds(start, LANES), :]
                rhs = jnp.concatenate(
                    [values, jnp.concatenate([values[:, :LANES], zero], axis=1)], axis=0
                )
                sum_ref[...] += sum_halves(dot(lhs, rhs))

            return carry

        lax.fori_loop(0, 9, block, 0)
        total = None
        for b in range(BASES):
            weight = mix_ref[b : b + 1, :] * math.exp(-0.5 * (b - MID) ** 2)
            term = sum_ref[b * CHUNK : (b + 1) * CHUNK, :] * weight
            total = term if total is None else total + term
        out_ref[pl.ds(start, CHUNK), :] = total
        return carry

    lax.fori_loop(0, CHUNKS, chunk, 0)


def silu(v):
    return v / (1.0 + jnp.exp(-v))


def stack_lanes(x):
    high, low = split(x)
    return jnp.concatenate([high, low, high], axis=1)


def final_body(
    feat_ref, pos_ref, msg_ref, in_ref, gain_ref, up_ref, down_ref, long_ref, again_ref, aup_ref, adown_ref, out_ref
):
    hats = Hats(pos_ref[...])
    up = stack_lanes(up_ref[...].T * gain_ref[...])
    down = stack_lanes(down_ref[...].T)
    at_atoms = jnp.zeros((ATOMS, LANES), F32)
    for r in range(0, ROWS, 2):
        cells = jnp.concatenate(
            [in_ref[pl.ds(r + k, LANES, stride=ROWS), :] for k in range(2)], axis=1
        )
        inverse = lax.rsqrt(jnp.mean(cells * cells, axis=0, keepdims=True) + 1e-06)
        hidden = silu(dot(up, stack_rows(cells * inverse)))
        mesh_out = dot(down, stack_rows(hidden))
        high, low = split(mesh_out)
        wh, wl = hats.two_rows(r)
        at_atoms = at_atoms + sum_halves(dot_nt(wh, jnp.concatenate([high, low], axis=0)))
        at_atoms = at_atoms + dot_nt(wl, high)
    summed = feat_ref[...] + msg_ref[...] + dot3(at_atoms, long_ref[...])
    inverse = lax.rsqrt(jnp.mean(summed * summed, axis=1, keepdims=True) + 1e-06)
    normed = summed * inverse * again_ref[...]
    hidden = silu(dot3(normed, aup_ref[...]))
    out_ref[...] = summed + dot3(hidden, adown_ref[...])


def whole():
    return pl.BlockSpec(memory_space=pltpu.VMEM)


def scalars():
    return pl.BlockSpec(memory_space=pltpu.SMEM)


def call(body, name, shape, in_specs, scratch, cost):
    return pl.pallas_call(
        body,
        out_shape=jax.ShapeDtypeStruct(shape, F32),
        in_specs=in_specs,
        out_specs=whole(),
        scratch_shapes=scratch,
        name=name,
        compiler_params=pltpu.CompilerParams(vmem_limit_bytes=LIMIT),
        cost_estimate=pl.CostEstimate(flops=cost, bytes_accessed=4 * 1024 * 1024, transcendentals=0),
    )


def pack_call(feat, pos, proj):
    return call(pack_body, "pack", (PACK, LANES), [whole()] * 3, [], 50_000_000)(feat, pos, proj)


def spread_call(feat, pos, proj):
    return call(spread_body, "spread", (LANES * ROWS, LANES), [whole()] * 3, [], 1_200_000_000)(
        feat, pos, proj
    )


def filter_call(screening, smearing, received):
    tables = [jnp.asarray(t) for t in filter_tables()]
    return call(
        filter_body,
        "filter",
        (LANES * ROWS, LANES),
        [scalars(), scalars()] + [whole()] * 7,
        [pltpu.VMEM((MESH * 32, LANES), F32), pltpu.VMEM((256, LANES), F32)],
        2_000_000_000,
    )(screening, smearing, received, *tables)


def short_call(live, near, left, right, mix):
    return call(
        short_body,
        "short_range",
        (ATOMS, LANES),
        [scalars()] + [whole()] * 4,
        [
            pltpu.VMEM((9, ATOMS + 64, 2 * LANES), BF),
            pltpu.VMEM((9, CHUNKS, 8, LANES), F32),
            pltpu.VMEM((3 * ATOMS, LANES), F32),
            pltpu.VMEM((BASES * CHUNK, LANES), F32),
        ],
        12_000_000_000,
    )(live, near, left, right, mix)


def final_call(feat, pos, msg, received, gain, up, down, long_proj, again, aup, adown):
    return call(final_body, "final", (ATOMS, LANES), [whole()] * 11, [], 2_400_000_000)(
        feat, pos, msg, received, gain, up, down, long_proj, again, aup, adown
    )


def passed_along(array, axis, by):
    count = lax.axis_size(axis)
    return lax.ppermute(array, axis, [(i, (i + by) % count) for i in range(count)])


def on_device(
    features,
    positions,
    tile_lists,
    value_proj,
    radial_mix,
    charge_proj,
    screening,
    smearing,
    mesh_gain,
    mesh_up,
    mesh_down,
    long_proj,
    atom_gain,
    atom_up,
    atom_down,
):
    feat, pos = features[0, 0], positions[0, 0]
    everyone = ("wide", "sixteen")
    spread = spread_call(feat, pos, charge_proj)
    packed = pack_call(feat, pos, value_proj)
    below = passed_along(packed, "sixteen", 1)
    above = passed_along(packed, "sixteen", -1)
    near = jnp.concatenate([below, packed, above], axis=0)
    left = passed_along(near, "wide", 1)
    right = passed_along(near, "wide", -1)
    received = lax.all_to_all(spread, everyone, split_axis=0, concat_axis=0, tiled=True)
    filtered = filter_call(screening, smearing, received)
    returned = lax.all_to_all(filtered, everyone, split_axis=0, concat_axis=0, tiled=True)
    codes = jnp.arange(36, dtype=jnp.int32)
    live = jnp.any(tile_lists[0, 0][:, :, None] == codes, axis=1).astype(jnp.int32)
    messages = short_call(live, near, left, right, radial_mix)
    updated = final_call(
        feat,
        pos,
        messages,
        returned,
        mesh_gain[None],
        mesh_up,
        mesh_down,
        long_proj,
        atom_gain[None],
        atom_up,
        atom_down,
    )
    return updated[None, None]


def solution(mesh):
    block = P("wide", "sixteen", None, None)
    channel = P(("wide", "sixteen"))
    in_specs = (block,) * 3 + (P(),) * 3 + (channel,) * 2 + (P(),) * 7
    return jax.shard_map(
        on_device, mesh=mesh, in_specs=in_specs, out_specs=block, check_vma=False
    )
```

profile of v0, /device:TPU:0, one launch (start us, length us, event | category | flops | bytes accessed | tf_op | source)
XLA Modules:
  0.0 104.0 jit_solution(6167270062563320006)
XLA Ops:
  0.0 0.7 copy.24
  0.7 0.9 copy-done
  1.6 0.8 copy-done.7
  2.5 3.8 %spread.1 = f32[3072,128]{1,0:T(8,128)} custom-call(f32[512,128]{1,0:T(8,128)S(1)} %bitcast.14, f32[3,512]{1,0:T(4,128)S(1)} %bitcast.17, f32[128,128]{1,0:T(8,128)S(1)} %copy-done.7), custom_call_target="tpu_custom_call" | custom-call | flops 1200000000 | bytes 4194304 | tf_op jit(solution)/shard_map/spread/pallas_call | solution.py:445
  6.3 11.1 %all-to-all-start = ((f32[128,24,128]{2,1,0:T(8,128)}), f32[128,24,128]{2,1,0:T(8,128)S(1)}, u32[]{:S(2)}, u32[]{:S(2)}) async-start(f32[128,24,128]{2,1,0:T(8,128)} %bitcast.2), calls=%async_computation | async-start | bytes 3145728 | tf_op jit(solution)/shard_map/all_to_all | solution.py:515
  17.7 1.1 %collective-permute-start = (f32[528,128]{1,0:T(8,128)S(1)}, f32[528,128]{1,0:T(8,128)S(1)}, u32[]{:S(2)}, u32[]{:S(2)}) collective-permute-start(f32[528,128]{1,0:T(8,128)S(1)} %pack.1), channel_id=1, source_target_pairs={{0,1},{1,2},{2,3},{3,4},{4,5},{5,6},{6,7},{7,8},{8,9},{9,10},{10,1... | collective-permute-start | bytes 811016 | tf_op jit(solution)/shard_map/ppermute | solution.py:486
  18.9 4.3 %collective-permute-start.1 = (f32[528,128]{1,0:T(8,128)S(1)}, f32[528,128]{1,0:T(8,128)S(1)}, u32[]{:S(2)}, u32[]{:S(2)}) collective-permute-start(f32[528,128]{1,0:T(8,128)S(1)} %pack.1), channel_id=1, source_target_pairs={{0,15},{1,0},{2,1},{3,2},{4,3},{5,4},{6,5},{7,6},{8,7},{9,8},{10,9... | collective-permute-start | bytes 811016 | tf_op jit(solution)/shard_map/ppermute | solution.py:486
  23.2 22.6 %collective-permute-done = f32[528,128]{1,0:T(8,128)S(1)} collective-permute-done((f32[528,128]{1,0:T(8,128)S(1)}, f32[528,128]{1,0:T(8,128)S(1)}, u32[]{:S(2)}, u32[]{:S(2)}) %collective-permute-start) | collective-permute-done | bytes 270368 | tf_op jit(solution)/shard_map/ppermute | solution.py:486
  45.8 2.9 %collective-permute-start.3 = (f32[1584,128]{1,0:T(8,128)S(1)}, f32[1584,128]{1,0:T(8,128)}, u32[]{:S(2)}, u32[]{:S(2)}) collective-permute-start(f32[1584,128]{1,0:T(8,128)S(1)} %pad_maximum_fusion.near_ref), channel_id=1, source_target_pairs={{0,112},{16,0},{32,16},{48,32},{64,48},{80,64},{96,80},{112,96},{1... | collective-permute-start | bytes 2433032 | tf_op jit(solution)/shard_map/ppermute | solution.py:486
  50.1 0.9 copy-done.12
  51.0 0.9 copy-done.13
  51.9 0.8 copy-done.16
  52.7 0.8 copy-done.17
  53.5 7.6 %filter.1 = f32[3072,128]{1,0:T(8,128)} custom-call(f32[1]{0:T(128)S(6)} %copy.25.screen_ref, f32[1]{0:T(128)S(6)} %copy.26.smear_ref, f32[3072,128]{1,0:T(8,128)S(1)} %bitcast.12, bf16[64,192]{1,0:T(8,128)(2,1)S(1)} %copy-done.14, bf16[128,96]{1,0:T(8,128)(2,1)S(1)} %copy-done.15, bf16[256,256]{1,0:T(8,128)(2,1)S(1)} %copy-done.12, ...), custom_call_target="tpu_custom_call" | custom-call | flops 2000000000 | bytes 4194304 | tf_op jit(solution)/shard_map/filter/pallas_call | solution.py:452
  61.1 5.0 %all-to-all-start.1 = ((f32[128,24,128]{2,1,0:T(8,128)}), f32[128,24,128]{2,1,0:T(8,128)S(1)}, u32[]{:S(2)}, u32[]{:S(2)}) async-start(f32[128,24,128]{2,1,0:T(8,128)} %bitcast.4), calls=%async_computation.1 | async-start | bytes 3145728 | tf_op jit(solution)/shard_map/all_to_all | solution.py:517
  66.2 13.3 %short_range.1.msg_ref = f32[512,128]{1,0:T(8,128)S(1)} custom-call(s32[4,36]{1,0:T(4,128)S(1)} %convert_element_type.3.live_ref, f32[1584,128]{1,0:T(8,128)S(1)} %pad_maximum_fusion.near_ref, f32[1584,128]{1,0:T(8,128)S(1)} %collective-permute-done.2.left_ref, f32[1584,128]{1,0:T(8,128)} %collective-permute-done.3.right_ref, f32[16,128]{1,0:T(8,128)S(1)} %copy-done.9), custom_call_target="tpu_custom_call" | custom-call | flops 12000000000 | bytes 4194304 | tf_op jit(solution)/shard_map/short_range/pallas_call | solution.py:463
  79.5 0.7 copy-done.18
  80.2 10.1 %all-to-all-done.1 = f32[128,24,128]{2,1,0:T(8,128)S(1)} async-done(((f32[128,24,128]{2,1,0:T(8,128)}), f32[128,24,128]{2,1,0:T(8,128)S(1)}, u32[]{:S(2)}, u32[]{:S(2)}) %all-to-all-start.1) | async-done | bytes 1572896 | tf_op jit(solution)/shard_map/all_to_all | solution.py:517
  90.3 0.9 copy-done.3
  91.2 0.9 copy-done.4
  92.1 0.9 copy-done.5
  93.0 0.9 copy-done.6
  93.9 0.9 copy-done.19
  94.9 9.1 %final.1 = f32[512,128]{1,0:T(8,128)} custom-call(f32[512,128]{1,0:T(8,128)S(1)} %bitcast.16, f32[3,512]{1,0:T(4,128)S(1)} %bitcast.19, f32[512,128]{1,0:T(8,128)S(1)} %copy-done.19, f32[3072,128]{1,0:T(8,128)S(1)} %bitcast.13, f32[1,128]{1,0:T(1,128)S(1)} %bitcast.20, f32[128,256]{1,0:T(8,128)S(1)} %copy-done.3, f32[256,128]{1,0:T(8,128)S(1)} %copy-done.4, ...), custom_call_target="tpu_custom_call" | custom-call | flops 2400000000 | bytes 4194304 | tf_op jit(solution)/shard_map/final/pallas_call | solution.py:479
  (39 shorter events, 0.5 us)
Async XLA Ops:
  0.7 0.9 copy-start
  1.6 0.8 copy-start.7
  6.3 11.2 %copy-start.1 = (f32[1,1,512,128]{3,2,1,0:T(8,128)S(1)}, f32[1,1,512,128]{3,2,1,0:T(8,128)}, u32[]{:S(2)}) copy-start(f32[1,1,512,128]{3,2,1,0:T(8,128)} %param.21) | copy-start | bytes 786436
  6.3 11.2 %copy-start.2 = (f32[128,128]{1,0:T(8,128)S(1)}, f32[128,128]{1,0:T(8,128)}, u32[]{:S(2)}) copy-start(f32[128,128]{1,0:T(8,128)} %proj_ref.2) | copy-start | bytes 196612
  6.3 43.8 %all-to-all-start = ((f32[128,24,128]{2,1,0:T(8,128)}), f32[128,24,128]{2,1,0:T(8,128)S(1)}, u32[]{:S(2)}, u32[]{:S(2)}) async-start(f32[128,24,128]{2,1,0:T(8,128)} %bitcast.2), calls=%async_computation | async-start | bytes 3145728 | tf_op jit(solution)/shard_map/all_to_all | solution.py:515
  17.5 32.6 %copy-start.14 = (bf16[64,192]{1,0:T(8,128)(2,1)S(1)}, bf16[64,192]{1,0:T(8,128)(2,1)}, u32[]{:S(2)}) copy-start(bf16[64,192]{1,0:T(8,128)(2,1)} %constant.14.clone.xf_ref) | copy-start | bytes 73732
  17.5 32.6 %copy-start.15 = (bf16[128,96]{1,0:T(8,128)(2,1)S(1)}, bf16[128,96]{1,0:T(8,128)(2,1)}, u32[]{:S(2)}) copy-start(bf16[128,96]{1,0:T(8,128)(2,1)} %constant.15.clone.yf_ref) | copy-start | bytes 73732
  17.7 28.0 %collective-permute-start = (f32[528,128]{1,0:T(8,128)S(1)}, f32[528,128]{1,0:T(8,128)S(1)}, u32[]{:S(2)}, u32[]{:S(2)}) collective-permute-start(f32[528,128]{1,0:T(8,128)S(1)} %pack.1), channel_id=1, source_target_pairs={{0,1},{1,2},{2,3},{3,4},{4,5},{5,6},{6,7},{7,8},{8,9},{9,10},{10,1... | collective-permute-start | bytes 811016 | tf_op jit(solution)/shard_map/ppermute | solution.py:486
  18.9 26.9 %collective-permute-start.1 = (f32[528,128]{1,0:T(8,128)S(1)}, f32[528,128]{1,0:T(8,128)S(1)}, u32[]{:S(2)}, u32[]{:S(2)}) collective-permute-start(f32[528,128]{1,0:T(8,128)S(1)} %pack.1), channel_id=1, source_target_pairs={{0,15},{1,0},{2,1},{3,2},{4,3},{5,4},{6,5},{7,6},{8,7},{9,8},{10,9... | collective-permute-start | bytes 811016 | tf_op jit(solution)/shard_map/ppermute | solution.py:486
  45.8 20.3 %collective-permute-start.2 = (f32[1584,128]{1,0:T(8,128)S(1)}, f32[1584,128]{1,0:T(8,128)S(1)}, u32[]{:S(2)}, u32[]{:S(2)}) collective-permute-start(f32[1584,128]{1,0:T(8,128)S(1)} %pad_maximum_fusion.near_ref), channel_id=1, source_target_pairs={{0,16},{16,32},{32,48},{48,64},{64,80},{80,96},{96,112},{112,0},{1... | collective-permute-start | bytes 2433032 | tf_op jit(solution)/shard_map/ppermute | solution.py:486
  45.8 20.3 %collective-permute-start.3 = (f32[1584,128]{1,0:T(8,128)S(1)}, f32[1584,128]{1,0:T(8,128)}, u32[]{:S(2)}, u32[]{:S(2)}) collective-permute-start(f32[1584,128]{1,0:T(8,128)S(1)} %pad_maximum_fusion.near_ref), channel_id=1, source_target_pairs={{0,112},{16,0},{32,16},{48,32},{64,48},{80,64},{96,80},{112,96},{1... | collective-permute-start | bytes 2433032 | tf_op jit(solution)/shard_map/ppermute | solution.py:486
  50.1 0.9 copy-start.12
  51.0 0.9 copy-start.13
  61.1 5.0 %copy-start.20 = (s32[1,1,4,16]{3,2,1,0:T(4,128)S(1)}, s32[1,1,4,16]{3,2,1,0:T(4,128)}, u32[]{:S(2)}) copy-start(s32[1,1,4,16]{3,2,1,0:T(4,128)} %param.23) | copy-start | bytes 772
  61.1 5.1 %copy-start.9 = (f32[16,128]{1,0:T(8,128)S(1)}, f32[16,128]{1,0:T(8,128)}, u32[]{:S(2)}) copy-start(f32[16,128]{1,0:T(8,128)} %mix_ref.1) | copy-start | bytes 24580
  61.1 29.2 %all-to-all-start.1 = ((f32[128,24,128]{2,1,0:T(8,128)}), f32[128,24,128]{2,1,0:T(8,128)S(1)}, u32[]{:S(2)}, u32[]{:S(2)}) async-start(f32[128,24,128]{2,1,0:T(8,128)} %bitcast.4), calls=%async_computation.1 | async-start | bytes 3145728 | tf_op jit(solution)/shard_map/all_to_all | solution.py:517
  66.1 24.2 %copy-start.8 = (f32[128,128]{1,0:T(8,128)S(1)}, f32[128,128]{1,0:T(8,128)}, u32[]{:S(2)}) copy-start(f32[128,128]{1,0:T(8,128)} %long_ref.1) | copy-start | bytes 196612
  66.1 24.2 %copy-start.10 = (f32[128]{0:T(128)S(1)}, f32[128]{0:T(128)}, u32[]{:S(2)}) copy-start(f32[128]{0:T(128)} %param.29) | copy-start | bytes 1540
  66.2 24.2 %copy-start.11 = (f32[128]{0:T(128)S(1)}, f32[128]{0:T(128)}, u32[]{:S(2)}) copy-start(f32[128]{0:T(128)} %param.33) | copy-start | bytes 1540
  90.3 0.9 copy-start.3
  91.2 0.9 copy-start.4
  92.1 0.9 copy-start.5
  93.0 0.9 copy-start.6
  93.9 0.9 copy-start.19
  (3 other events, 2.2 us)
where the time goes:
time: 105 us; the launch traced here: 104 us
  Pallas kernels  34 us (32%)
  waiting for transfers between devices  32.7 us (31%)
  starting transfers between devices  24.5 us (23%)
  local copies, waits for them, and re-layouts  11.1 us (11%)
  between operations  1.5 us (1%)
    ppermute x4, waiting for transfers between devices, passed_along(): lax.ppermute(array, axis, [(i, (i + by) % count) for i in range(count)])  22.6 us
    pallas_call x1, Pallas kernels, short_call(): call(short_body, 'short_range', (ATOMS, LANES), [scalars()] + [whole()] *...  13.3 us
    all_to_all x1, starting transfers between devices, on_device(): lax.all_to_all(spread, everyone, split_axis=0, concat_axis=0, tiled=True)  11.1 us
    unnamed x43, local copies, waits for them, and re-layouts  11.1 us
    all_to_all x1, waiting for transfers between devices, on_device(): lax.all_to_all(filtered, everyone, split_axis=0, concat_axis=0, tiled=True)  10.1 us
    pallas_call x1, Pallas kernels, final_call(): call(final_body, 'final', (ATOMS, LANES), [whole()] * 11, [], 2400000000)  9.08 us
    ppermute x4, starting transfers between devices, passed_along(): lax.ppermute(array, axis, [(i, (i + by) % count) for i in range(count)])  8.37 us
    pallas_call x1, Pallas kernels, filter_call(): call(filter_body, 'filter', (LANES * ROWS, LANES), [scalars(), scalars()]...  7.61 us
  transfers between devices with their start and end apart: 6, of which 2 were waited for; matrix products, arithmetic and copies ran while one was open for 0% of the time, Pallas kernels for 20%

commit v1 on v0

v1 whole, which is shorter than its diff:
```python
import functools
import math

import jax
import jax.numpy as jnp
import ml_dtypes
import numpy as np
from jax import lax
from jax.experimental import pallas as pl
from jax.experimental.pallas import tpu as pltpu
from jax.sharding import PartitionSpec as P

F32 = jnp.float32
BF = jnp.bfloat16
MESH = 64
LANES = 128
ATOMS = 512
CHUNK = 64
CHUNKS = ATOMS // CHUNK
BASES = 16
ROWS = 24
PACK = 528
FAR = 1000.0
CUTOFF = 0.05
MID = 8
LIMIT = 32 * 1024 * 1024
SHORT_COST = 12_000_000_000
PREPARE_COST = 1_000


def split(x):
    hi = x.astype(BF)
    return hi, (x - hi.astype(F32)).astype(BF)


def dot(a, b):
    return jnp.dot(a, b, preferred_element_type=F32)


def dot_nt(a, b):
    return lax.dot_general(a, b, (((1,), (1,)), ((), ())), preferred_element_type=F32)


def dot3(a, b):
    ah, al = split(a)
    bh, bl = split(b)
    return dot(ah, bh) + (dot(ah, bl) + dot(al, bh))


def rows_of(pos_ref):
    return jnp.concatenate([pos_ref[0], pos_ref[1], pos_ref[2]], axis=0)


def lane_iota(shape):
    return lax.broadcasted_iota(jnp.int32, shape, len(shape) - 1)


def half_turn(x):
    return pltpu.roll(x, 64, x.ndim - 1)


def pack_body(feat_a, pos_a, feat_b, pos_b, feat_c, pos_c, proj_ref, out_ref):
    proj = proj_ref[...]
    for k, (feat, pos_ref) in enumerate(((feat_a, pos_a), (feat_b, pos_b), (feat_c, pos_c))):
        base = k * PACK
        out_ref[base : base + ATOMS, :] = dot3(feat[...], proj)
        for d in range(3):
            pos = pos_ref[d]
            for t in range(4):
                row = base + ATOMS + 4 * d + t
                out_ref[row : row + 1, :] = pos[:, t * LANES : (t + 1) * LANES]
        out_ref[base + ATOMS + 12 : base + PACK, :] = jnp.zeros((PACK - ATOMS - 12, LANES), F32)


def hat(distance):
    return jnp.maximum(1.0 - jnp.abs(distance), 0.0)


def planes_of(uy, uz, half, z, low):
    depth = jnp.abs(uz - z)
    hz = hat(jnp.minimum(depth, 64.0 - depth))
    top = jnp.where(low, hat(uy - 4.0) * hz, 0.0)
    return [hat(uy - half) * hz, hat(uy - 2.0 - half) * hz, top]


def planes_across(pos):
    filled = jnp.concatenate([pos, jnp.zeros((5, ATOMS), F32)], axis=0)
    columns = filled.T
    wide = lambda d, scale: jnp.broadcast_to(columns[:, d : d + 1] * scale, (ATOMS, LANES))
    lane = lane_iota((1, LANES))
    half, z = (lane // 64).astype(F32), (lane % 64).astype(F32)
    return jnp.concatenate(planes_of(wide(1, 4.0), wide(2, float(MESH)), half, z, lane < 64), axis=1)


def planes_down(pos):
    row = lax.broadcasted_iota(jnp.int32, (LANES, 1), 0)
    half, z = (row // 64).astype(F32), (row % 64).astype(F32)
    uy, uz = pos[1:2, :] * 4.0, pos[2:3, :] * float(MESH)
    return jnp.concatenate(planes_of(uy, uz, half, z, row < 64), axis=0)


def spread_body(feat_ref, pos_ref, proj_ref, out_ref):
    pos = rows_of(pos_ref)
    wh, wl = split(planes_across(pos))
    ux = pos[0:1, :] * 8.0
    charges = dot3(feat_ref[...], proj_ref[...]).T
    highs, lows = [], []
    for x in range(9):
        high, low = split(charges * hat(ux - float(x)))
        highs.append(high)
        lows.append(low)
    high = jnp.concatenate(highs, axis=0)
    low = jnp.concatenate(lows, axis=0)
    result = dot(high, wh) + (dot(low, wh) + dot(high, wl))
    piece = lambda x, k: result[x * LANES : (x + 1) * LANES, k * LANES : (k + 1) * LANES]
    edge = [half_turn(piece(8, 0)), piece(8, 0), half_turn(piece(8, 1)), piece(8, 1), half_turn(piece(8, 2))]
    below = lane_iota((1, LANES)) < 64
    for x in range(8):
        out_ref[pl.ds(x, LANES, stride=ROWS), :] = piece(x, 0)
        out_ref[pl.ds(8 + x, LANES, stride=ROWS), :] = piece(x, 1)
        top = piece(x, 2)
        out_ref[pl.ds(16 + x, LANES, stride=ROWS), :] = jnp.where(below, top, edge[x]) if x < 5 else top


def real_basis():
    n = np.arange(MESH)
    rows = []
    for k in range(MESH):
        if k == 0:
            rows.append(np.full(MESH, 1.0 / 8.0))
        elif k == MESH // 2:
            rows.append(np.where(n % 2 == 0, 1.0, -1.0) / 8.0)
        elif k < MESH // 2:
            rows.append(np.cos(2 * np.pi * (k * n % MESH) / MESH) * math.sqrt(2.0) / 8.0)
        else:
            rows.append(np.sin(2 * np.pi * ((MESH - k) * n % MESH) / MESH) * math.sqrt(2.0) / 8.0)
    return np.stack(rows)


def halves(table):
    high = table.astype(np.float32).astype(ml_dtypes.bfloat16)
    low = (table - high.astype(np.float64)).astype(np.float32).astype(ml_dtypes.bfloat16)
    return high, low


def stacked(table):
    high, low = halves(table)
    return np.concatenate([high, low, high], axis=1)


def squared(table):
    high, low = halves(table)
    top = np.concatenate([high, low], axis=1)
    bottom = np.concatenate([high, np.zeros_like(low)], axis=1)
    return np.concatenate([top, bottom], axis=0)


def filter_tables():
    q = real_basis()
    y_forward = np.concatenate([q[:, 0::2], q[:, 1::2]], axis=0)
    y_back = np.concatenate([q.T[0::2], q.T[1::2]], axis=0)
    twice = np.kron(np.eye(2), q.T)
    tables = [stacked(q), stacked(y_forward), squared(twice), squared(twice.T), stacked(y_back), stacked(q.T)]
    wide = 2 * LANES
    filled = [np.pad(t.astype(np.float32), ((0, 0), (0, wide - t.shape[1]))) for t in tables]
    return np.concatenate(filled, axis=0).astype(ml_dtypes.bfloat16)


def stack_rows(x):
    high, low = split(x)
    return jnp.concatenate([high, high, low], axis=0)


def sum_halves(x):
    return x[:, :LANES] + x[:, LANES:]


def filter_body(
    screen_ref, smear_ref, in_ref, table_ref, out_ref, turn_ref, edge_ref
):
    devices = 128
    low = lane_iota((1, LANES)) < 64
    place = lax.broadcasted_iota(jnp.int32, (devices, 1), 0) % 16

    side = [in_ref[pl.ds(16 + y, devices, stride=ROWS), :] for y in range(5)]
    corner = jnp.where(place == 0, pltpu.roll(side[4], 113, 0), pltpu.roll(side[4], 1, 0))
    side[0] = side[0] + corner
    for h in range(2):
        both = jnp.where(low, half_turn(side[2 * h]), side[2 * h + 1])
        edge_ref[h * devices : (h + 1) * devices, :] = pltpu.roll(both, 16, 0)

    first_row = lax.broadcasted_iota(jnp.int32, (8, 1), 0) == 0
    x_forward = table_ref[0:64, 0:192]
    for s in range(0, 16, 2):
        parts = []
        for k in range(4):
            d, h = s + k // 2, k % 2
            tiles = []
            for w in range(8):
                at = w * 16 + d
                tile = in_ref[at * ROWS + h * 8 : at * ROWS + h * 8 + 8, :]
                edge = edge_ref[h * devices + at : h * devices + at + 1, :]
                tile = tile + jnp.where(first_row, edge, 0.0)
                if h == 0:
                    below = (w * 16 + (d + 15) % 16) * ROWS + 16
                    tile = tile + jnp.where(low, in_ref[below : below + 8, :], 0.0)
                tiles.append(tile)
            parts.append(jnp.concatenate(tiles, axis=0))
        result = dot(x_forward, stack_rows(jnp.concatenate(parts, axis=1)))
        for k in range(4):
            turn_ref[pl.ds(2 * s + k, MESH, stride=32), :] = result[:, k * LANES : (k + 1) * LANES]

    kappa = screen_ref[0]
    kappa_sq = kappa * kappa
    decay = -0.5 * smear_ref[0] * smear_ref[0]
    lane = lane_iota((1, LANES))
    fold = lambda k: jnp.minimum(k, MESH - k).astype(F32)
    nz = fold(lane % 64)
    ny = fold(lax.broadcasted_iota(jnp.int32, (MESH, 1), 0))
    scale = 4.0 * math.pi**2
    yz = (ny * ny + nz * nz) * scale
    y_forward, z_forward = table_ref[64:192, 0:96], table_ref[192:448, :]
    z_back, y_back = table_ref[448:704, :], table_ref[704:768, 0:192]
    group = 32
    for start in range(0, 32, group):
        planes = []
        for p in range(start, start + group, 2):
            pairs = jnp.concatenate(
                [turn_ref[(2 * p + k) * 32 : (2 * p + k + 1) * 32, :] for k in range(4)], axis=1
            )
            result = dot(y_forward, stack_rows(pairs))
            for k in range(2):
                a = result[:, 2 * k * LANES : (2 * k + 1) * LANES]
                b = result[:, (2 * k + 1) * LANES : (2 * k + 2) * LANES]
                straight = jnp.where(low, a[:MESH], b[MESH:])
                planes.append(straight + half_turn(jnp.where(low, b[:MESH], a[MESH:])))
        stack = jnp.concatenate(planes, axis=0)
        stack = sum_halves(dot(jnp.concatenate(split(stack), axis=1), z_forward))
        gains = []
        for p in range(start, start + group):
            nx = fold(2 * p + lane // 64)
            square = yz + nx * nx * scale
            gains.append(kappa_sq * jnp.exp(square * decay) / (square + kappa_sq))
        stack = stack * jnp.concatenate(gains, axis=0)
        stack = sum_halves(dot(jnp.concatenate(split(stack), axis=1), z_back))
        for g in range(0, group, 4):
            pair = jnp.concatenate([stack[(g + k) * MESH : (g + k + 1) * MESH] for k in range(4)], axis=1)
            result = dot(y_back, stack_rows(pair))
            for k in range(4):
                p = start + g + k
                a = result[:32, k * LANES : (k + 1) * LANES]
                b = result[32:, k * LANES : (k + 1) * LANES]
                turn_ref[2 * p * 32 : 2 * p * 32 + 32, :] = jnp.where(low, a, half_turn(b))
                turn_ref[2 * p * 32 + 32 : 2 * p * 32 + 64, :] = jnp.where(low, half_turn(a), b)

    x_back = table_ref[768:832, 0:192]
    for s in range(0, 16, 2):
        pair = jnp.concatenate(
            [turn_ref[pl.ds(2 * s + k, MESH, stride=32), :] for k in range(4)], axis=1
        )
        result = dot(x_back, stack_rows(pair))
        for w in range(8):
            for k in range(4):
                d, h = s + k // 2, k % 2
                at = (w * 16 + d) * ROWS
                tile = result[w * 8 : (w + 1) * 8, k * LANES : (k + 1) * LANES]
                out_ref[at + h * 8 : at + h * 8 + 8, :] = tile
                if h == 0:
                    below = (w * 16 + (d + 15) % 16) * ROWS + 16
                    out_ref[below : below + 8, :] = jnp.where(low, tile, 0.0)

    ahead = [pltpu.roll(out_ref[pl.ds(8 * h, devices, stride=ROWS), :], 112, 0) for h in range(2)]
    turned = [half_turn(x) for x in ahead]
    corner = jnp.where(place == 15, pltpu.roll(turned[0], 15, 0), pltpu.roll(turned[0], 127, 0))
    for y, high in enumerate([turned[0], ahead[0], turned[1], ahead[1], corner]):
        rows = pl.ds(16 + y, devices, stride=ROWS)
        out_ref[rows, :] = jnp.where(low, out_ref[rows, :], high)


ENVELOPE = (
    0.9999999991137324,
    -0.4674010362718563,
    0.0945531128786198,
    -0.011119339660821159,
    0.0008600612678157039,
    -4.252312938118321e-05,
)


def short_body(
    blocks, units, live_ref, pos_ref, part_ref, mix_ref, *rest
):
    *packs, out_ref, val_ref, win_ref, own_ref = rest
    lane = lane_iota((1, LANES))
    filled = jnp.concatenate([rows_of(pos_ref), jnp.zeros((5, ATOMS), F32)], axis=0)
    columns = filled.T
    for d, scale in ((0, 0.125), (1, 0.0625), (2, 1.0)):
        own_ref[d * ATOMS : (d + 1) * ATOMS, :] = jnp.broadcast_to(
            columns[:, d : d + 1] * scale, (ATOMS, LANES)
        )

    row = lax.broadcasted_iota(jnp.int32, (16, 1), 0)
    axis, tile = row // 4, row % 4
    pick = lambda x, y, z: jnp.where(axis == 0, x, jnp.where(axis == 1, y, z))
    scale = pick(0.125, 0.0625, 1.0)
    wrap_low = jnp.where((axis == 2) & (tile == 0), -1.0, 0.0)
    wrap_high = jnp.where((axis == 2) & (tile == 3), 1.0, 0.0)
    for k, nb in enumerate(blocks):
        dx, dy = nb // 3 - 1, nb % 3 - 1
        ref, base = packs[0 if dx < 1 else -1], (dy + 1) * PACK
        high, low = split(ref[base : base + ATOMS, :])
        both = jnp.concatenate([high, low], axis=1)
        val_ref[k, 32 : 32 + ATOMS, :] = both
        val_ref[k, 0:32, :] = both[ATOMS - 32 :, :]
        val_ref[k, ATOMS + 32 :, :] = both[:32, :]
        pos = (ref[base + ATOMS : base + PACK, :] + pick(float(dx), float(dy), 0.0)) * scale
        up = pltpu.roll(pos, 32, 1)
        before = jnp.where(tile == 0, pltpu.roll(up, 13, 0), pltpu.roll(up, 1, 0)) + wrap_low
        win_ref[k, 0] = jnp.where(lane < 32, before, up)
        down = pltpu.roll(pos, 96, 1)
        after = jnp.where(tile == 3, pltpu.roll(down, 3, 0), pltpu.roll(down, 15, 0)) + wrap_high
        win_ref[k, 1] = jnp.where(lane < 96, down, after)

    me = lax.broadcasted_iota(jnp.int32, (CHUNK, LANES), 0) + 32
    itself = (me == lane_iota((CHUNK, LANES))).astype(F32)
    zero = jnp.zeros((LANES, LANES), BF)
    half = BASES // 2

    def chunk(acc_a, acc_b, m, carry):
        t = m // 2
        parity = m % 2
        even = parity == 0
        tile_a = jnp.where(even, (t + 3) % 4, t)
        tile_b = jnp.where(even, t, (t + 1) % 4)
        from_first = lane < jnp.where(even, 32, 96)
        start = pl.multiple_of(m * CHUNK, CHUNK)

        for k, nb in enumerate(blocks):
            live_a = live_ref[t, nb * 4 + tile_a]
            live_b = live_ref[t, nb * 4 + tile_b]

            @pl.when(live_a + live_b > 0)
            def _(k=k, nb=nb, live_a=live_a, live_b=live_b):
                values = val_ref[k, pl.ds(start, LANES), :]
                rhs = jnp.concatenate(
                    [values, jnp.concatenate([values[:, :LANES], zero], axis=1)], axis=0
                )
                for unit in range(2):
                    pltpu.matmul_push_rhs(rhs, 0, unit)
                far_a = (1 - live_a).astype(F32) * FAR
                far_b = (1 - live_b).astype(F32) * FAR
                take = lambda d: win_ref[k, parity, pl.ds(4 * d + t, 1), :]
                xj = take(0) + jnp.where(from_first, far_a, far_b)
                dx = xj - own_ref[pl.ds(start, CHUNK), :]
                dy = take(1) - own_ref[pl.ds(ATOMS + start, CHUNK), :]
                dz = take(2) - own_ref[pl.ds(2 * ATOMS + start, CHUNK), :]
                s = (dx * dx + dy * dy + dz * dz) * (1.0 / CUTOFF**2)
                if nb == 4:
                    s = jnp.maximum(s, itself)
                s = jnp.minimum(s, 1.0)
                q = s * lax.rsqrt(jnp.maximum(s, 1e-30))
                v = q * float(BASES - 1) - float(MID)
                env = jnp.full_like(s, ENVELOPE[-1])
                for c in ENVELOPE[-2::-1]:
                    env = env * s + c
                rest = 1.0 - s
                middle = jnp.exp(-0.5 * v * v) * (env * (rest * rest))
                up, down = jnp.exp(v), jnp.exp(-v)
                terms = [None] * BASES
                terms[MID] = middle
                for b in range(MID + 1, BASES):
                    terms[b] = terms[b - 1] * up
                for b in range(MID - 1, -1, -1):
                    terms[b] = terms[b + 1] * down
                sides = [jnp.concatenate(split(x), axis=1) for x in terms]
                pltpu.matmul_acc_lhs(acc_a, jnp.concatenate(sides[:half], axis=0), load_staged_rhs=0)
                pltpu.matmul_acc_lhs(acc_b, jnp.concatenate(sides[half:], axis=0), load_staged_rhs=0)

        total = part_ref[pl.ds(start, CHUNK), :]
        for unit, acc in enumerate((acc_a, acc_b)):
            found = sum_halves(pltpu.matmul_pop(acc))
            for j in range(half):
                b = unit * half + j
                weight = mix_ref[b : b + 1, :] * math.exp(-0.5 * (b - MID) ** 2)
                total = total + found[j * CHUNK : (j + 1) * CHUNK, :] * weight
        out_ref[pl.ds(start, CHUNK), :] = total
        return carry

    pl.run_scoped(
        lambda acc_a, acc_b: lax.fori_loop(0, CHUNKS, functools.partial(chunk, acc_a, acc_b), 0), *units
    )


def silu(v):
    half = 0.5 * v
    return half + half * jnp.tanh(half)


def stack_lanes(x):
    high, low = split(x)
    return jnp.concatenate([high, low, high], axis=1)


def beside(x):
    return jnp.concatenate(split(x), axis=1)


def prepare_body(pos_ref, gain_ref, up_ref, down_ref, long_ref, again_ref, aup_ref, adown_ref, out_ref, hat_out):
    out_ref[0:256, 0:384] = stack_lanes(up_ref[...].T * gain_ref[...])
    down = stack_lanes(down_ref[...].T)
    out_ref[256:384, :] = down[:, :512]
    out_ref[384:512, 0:256] = down[:, 512:]
    out_ref[1536:1664, :] = beside((aup_ref[...].T * again_ref[...]).T)
    out_ref[1664:1920, 0:256] = beside(adown_ref[...])
    out_ref[384:512, 256:512] = beside(long_ref[...])
    pos = rows_of(pos_ref)
    high, low = split(planes_down(pos))
    main = 2 * LANES
    pieces = [high[:main], high[:main], low[:main], high[main : main + 64], high[main : main + 64], low[main:]]
    out_ref[512:1536, :] = jnp.concatenate(pieces, axis=0)
    ux = pos[0:1, :] * 8.0
    hats = [hat(ux - float(x)) for x in range(9)] + [jnp.zeros((7, ATOMS), F32)]
    hat_out[...] = jnp.concatenate(hats, axis=0)


def dot_beside(x, pair):
    high, low = split(x)
    width = pair.shape[1] // 2
    wide = dot(high, pair)
    return wide[:, :width] + (wide[:, width:] + dot(low, pair[:, :width]))


def final_body(msg_ref, in_ref, set_ref, hat_ref, out_ref):
    up = set_ref[0:256, 0:384]
    down = jnp.concatenate([set_ref[256:384, :], set_ref[384:512, 0:256]], axis=1)
    mesh_out = []
    width = 12
    for r in range(0, ROWS, width):
        cells = jnp.concatenate(
            [in_ref[pl.ds(r + k, LANES, stride=ROWS), :] for k in range(width)], axis=1
        )
        inverse = lax.rsqrt(jnp.mean(cells * cells, axis=0, keepdims=True) + 1e-06)
        hidden = silu(dot(up, stack_rows(cells * inverse)))
        result = dot(down, stack_rows(hidden))
        mesh_out += [result[:, k * LANES : (k + 1) * LANES] for k in range(width)]
    below = lane_iota((1, LANES)) < 64
    top = mesh_out[16:]
    mixed = lambda a, b: jnp.where(below, half_turn(a), b)
    edge = [mixed(top[0], top[1]), mixed(top[2], top[3]), half_turn(top[4])]
    stacks = []
    for x in range(9):
        first, second, last = edge if x == 8 else [mesh_out[x], mesh_out[8 + x], top[x]]
        high, low = split(jnp.concatenate([first, second], axis=1))
        rounded = last.astype(BF).astype(F32)
        both = jnp.where(below, rounded, half_turn(last - rounded))
        stacks.append(jnp.concatenate([high, low, high, both.astype(BF), rounded.astype(BF)], axis=1))
    found = dot(jnp.concatenate(stacks, axis=0), set_ref[512:1536, :])
    total = None
    for x in range(9):
        term = found[x * LANES : (x + 1) * LANES] * hat_ref[x : x + 1, :]
        total = term if total is None else total + term
    summed = msg_ref[...] + dot_beside(total.T, set_ref[384:512, 256:512])
    inverse = lax.rsqrt(jnp.mean(summed * summed, axis=1, keepdims=True) + 1e-06)
    hidden = silu(dot_beside(summed * inverse, set_ref[1536:1664, :]))
    out_ref[...] = summed + dot_beside(hidden, set_ref[1664:1920, 0:256])


def whole():
    return pl.BlockSpec(memory_space=pltpu.VMEM)


def scalars():
    return pl.BlockSpec(memory_space=pltpu.SMEM)


def in_hbm(x):
    return pltpu.with_memory_space_constraint(x, pltpu.HBM)


def remote():
    return pl.BlockSpec(memory_space=pltpu.HBM)


class Fetched:
    def __init__(self, source, target, semaphore, first, cuts):
        self.target = target
        self.copies = []
        for k, (low, high) in enumerate(zip(cuts[:-1], cuts[1:])):
            rows = pl.ds(low, high - low)
            copy = pltpu.make_async_copy(source.at[rows], target.at[rows], semaphore.at[first + k])
            copy.start()
            self.copies.append([low, high, copy])

    def __getitem__(self, index):
        rows = index[0] if isinstance(index, tuple) else index
        if isinstance(rows, slice):
            start, stop = rows.start or 0, self.target.shape[0] if rows.stop is None else rows.stop
        elif isinstance(rows, int):
            start, stop = rows, rows + 1
        else:
            start, stop = 0, self.target.shape[0]
        for entry in self.copies:
            if entry[2] is not None and entry[0] < stop and entry[1] > start:
                entry[2].wait()
                entry[2] = None
        return self.target[index]


def call(body, name, shapes, places, scratch, cost, operands, cuts={}):
    specs = {"v": whole, "s": scalars, "h": remote}
    far = [i for i, p in enumerate(places) if p == "h"]
    buffers = [pltpu.VMEM(operands[i].shape, operands[i].dtype) for i in far]
    count = len(places)
    parts = [cuts.get(i, (0, operands[i].shape[0])) for i in far]
    firsts = [sum(len(p) - 1 for p in parts[:k]) for k in range(len(far) + 1)]

    def kernel(*refs):
        inputs, rest = list(refs[:count]), refs[count:]
        if far:
            held, semaphores = rest[-len(far) - 1 : -1], rest[-1]
            for k, i in enumerate(far):
                inputs[i] = Fetched(inputs[i], held[k], semaphores, firsts[k], parts[k])
            rest = rest[: -len(far) - 1]
        body(*inputs, *rest)

    extra = buffers + [pltpu.SemaphoreType.DMA((firsts[-1],))] if far else []
    return pl.pallas_call(
        kernel,
        out_shape=[jax.ShapeDtypeStruct(x, F32) if isinstance(x, tuple) else x for x in shapes],
        in_specs=[specs[p]() for p in places],
        out_specs=[whole()] * len(shapes),
        scratch_shapes=list(scratch) + extra,
        name=name,
        compiler_params=pltpu.CompilerParams(vmem_limit_bytes=LIMIT),
        cost_estimate=pl.CostEstimate(flops=cost, bytes_accessed=4 * 1024 * 1024, transcendentals=0),
    )(*operands)


def pack_call(*operands):
    return call(pack_body, "pack", [(3 * PACK, LANES)], "vvvvvvv", [], 12_000_000_000, operands)[0]


def spread_call(feat, pos, proj):
    operands = [in_hbm(x) for x in (feat, pos, proj)]
    return call(spread_body, "spread", [(LANES * ROWS, LANES)], "hhh", [], 1_200_000_000, operands)[0]


def prepare_call(*operands):
    shapes = [jax.ShapeDtypeStruct((1920, 512), BF), (16, ATOMS)]
    return call(prepare_body, "prepare", shapes, "v" * 8, [], PREPARE_COST, operands)


def filter_call(screening, smearing, received):
    scratch = [pltpu.VMEM((MESH * 32, LANES), F32), pltpu.VMEM((256, LANES), F32)]
    operands = (screening, smearing, received, in_hbm(jnp.asarray(filter_tables())))
    shapes = [(LANES * ROWS, LANES)]
    cuts = {3: (0, 64, 832)}
    return call(filter_body, "filter", shapes, "ssvh", scratch, 2_000_000_000, operands, cuts)[0]


def short_call(mesh, blocks, *operands):
    with jax.sharding.use_abstract_mesh(mesh.abstract_mesh):
        units = [pltpu.ACC(i)((BASES // 2 * CHUNK, 2 * LANES), F32) for i in range(2)]
    scratch = [
        pltpu.VMEM((len(blocks), ATOMS + 64, 2 * LANES), BF),
        pltpu.VMEM((len(blocks), 2, 16, LANES), F32),
        pltpu.VMEM((3 * ATOMS, LANES), F32),
    ]
    body = functools.partial(short_body, blocks, units)
    places = "s" + "v" * (len(operands) - 1)
    return call(body, "short_range", [(ATOMS, LANES)], places, scratch, SHORT_COST, operands)[0]


def final_call(messages, returned, weights, hats):
    operands = (messages, returned, in_hbm(weights), in_hbm(hats))
    cuts = {2: (0, 512, 1536, 1920)}
    return call(final_body, "final", [(ATOMS, LANES)], "vvhh", [], 2_400_000_000, operands, cuts)[0]


def passed_along(array, axis, by):
    count = lax.axis_size(axis)
    return lax.ppermute(array, axis, [(i, (i + by) % count) for i in range(count)])


def on_device(
    mesh,
    features,
    positions,
    tile_lists,
    value_proj,
    radial_mix,
    charge_proj,
    screening,
    smearing,
    mesh_gain,
    mesh_up,
    mesh_down,
    long_proj,
    atom_gain,
    atom_up,
    atom_down,
):
    feat, pos = features[0, 0], positions.reshape(3, 1, ATOMS)
    everyone = ("wide", "sixteen")
    feat_below = passed_along(feat, "sixteen", 1)
    feat_above = passed_along(feat, "sixteen", -1)
    pos_below = passed_along(pos, "sixteen", 1)
    pos_above = passed_along(pos, "sixteen", -1)
    spread = spread_call(feat, pos, charge_proj)
    received = lax.all_to_all(spread, everyone, split_axis=0, concat_axis=0, tiled=True)
    near = pack_call(feat_below, pos_below, feat, pos, feat_above, pos_above, value_proj)
    left = passed_along(near, "wide", 1)
    right = passed_along(near, "wide", -1)
    codes = jnp.arange(36, dtype=jnp.int32)
    live = jnp.any(tile_lists[0, 0][:, :, None] == codes, axis=1).astype(jnp.int32)
    prepared = prepare_call(
        pos, mesh_gain[None], mesh_up, mesh_down, long_proj, atom_gain[None], atom_up, atom_down
    )
    part = short_call(mesh, (3, 4, 5), live, pos, feat, radial_mix, near)
    received, part = lax.optimization_barrier((received, part))
    filtered = filter_call(screening, smearing, received)
    returned = lax.all_to_all(filtered, everyone, split_axis=0, concat_axis=0, tiled=True)
    messages = short_call(mesh, (0, 1, 2, 6, 7, 8), live, pos, part, radial_mix, left, right)
    updated = final_call(messages, returned, *prepared)
    return updated[None, None]


def solution(mesh):
    block = P("wide", "sixteen", None, None)
    channel = P(("wide", "sixteen"))
    in_specs = (block,) * 3 + (P(),) * 3 + (channel,) * 2 + (P(),) * 7
    return jax.shard_map(
        functools.partial(on_device, mesh), mesh=mesh, in_specs=in_specs, out_specs=block, check_vma=False
    )
```

time: 105 us -> 88.4 us (0.84)
  local copies, waits for them, and re-layouts: 11.1 us -> 1.98 us
  waiting for transfers between devices: 32.7 us -> 26.2 us
    ppermute x4 -> x6, waiting for transfers between devices: 22.6 us -> 0.02 us  [passed_along(): lax.ppermute(array, axis, [(i, (i + by) % count) for i in range(count)])]
    all_to_all x1, waiting for transfers between devices: 0.01 us -> 13.6 us  [on_device(): lax.all_to_all(spread, everyone, split_axis=0, concat_axis=0, tiled=True)]
    unnamed x43 -> x28, local copies, waits for them, and re-layouts: 11.1 us -> 1.98 us
    ppermute x4 -> x6, starting transfers between devices: 8.37 us -> 14.9 us  [passed_along(): lax.ppermute(array, axis, [(i, (i + by) % count) for i in range(count)])]
    all_to_all x1, starting transfers between devices: 11.1 us -> 4.96 us  [on_device(): lax.all_to_all(spread, everyone, split_axis=0, concat_axis=0, tiled=True)]
    all_to_all x1, waiting for transfers between devices: 10.1 us -> 12.5 us  [on_device(): lax.all_to_all(filtered, everyone, split_axis=0, concat_axis=0, tiled=True)]
    pallas_call x5 -> x7, Pallas kernels: 34 us -> 33.3 us  [call(): pl.pallas_call(kernel, out_shape=[jax.ShapeDtypeStruct(x, F32) if isinsta...]
  transfers between devices with their start and end apart: 6 -> 8, of which waited for: 2 -> 2; matrix products, arithmetic and copies ran while one was open for 0% -> 0% of each run, Pallas kernels for 20% -> 30%
where the time goes in v1:
time: 88.4 us; the launch traced here: 88.1 us
  Pallas kernels  33.3 us (38%)
  waiting for transfers between devices  26.2 us (30%)
  starting transfers between devices  24.8 us (28%)
  local copies, waits for them, and re-layouts  1.98 us (2%)
  between operations  1.76 us (2%)
    pallas_call x7, Pallas kernels, call(): pl.pallas_call(kernel, out_shape=[jax.ShapeDtypeStruct(x, F32) if isinsta...  33.3 us
    ppermute x6, starting transfers between devices, passed_along(): lax.ppermute(array, axis, [(i, (i + by) % count) for i in range(count)])  14.9 us
    all_to_all x1, waiting for transfers between devices, on_device(): lax.all_to_all(spread, everyone, split_axis=0, concat_axis=0, tiled=True)  13.6 us
    all_to_all x1, waiting for transfers between devices, on_device(): lax.all_to_all(filtered, everyone, split_axis=0, concat_axis=0, tiled=True)  12.5 us
    all_to_all x1, starting transfers between devices, on_device(): lax.all_to_all(filtered, everyone, split_axis=0, concat_axis=0, tiled=True)  4.97 us
    all_to_all x1, starting transfers between devices, on_device(): lax.all_to_all(spread, everyone, split_axis=0, concat_axis=0, tiled=True)  4.96 us
    unnamed x28, local copies, waits for them, and re-layouts  1.98 us
  transfers between devices with their start and end apart: 8, of which 2 were waited for; matrix products, arithmetic and copies ran while one was open for 0% of the time, Pallas kernels for 30%

profile of v1, /device:TPU:0, one launch (start us, length us, event | category | flops | bytes accessed | tf_op | source)
XLA Modules:
  0.0 88.1 jit_solution(5065775870496689209)
XLA Ops:
  0.0 2.0 %collective-permute-start = (f32[512,128]{1,0:T(8,128)}, f32[512,128]{1,0:T(8,128)S(1)}, u32[]{:S(2)}, u32[]{:S(2)}) collective-permute-start(f32[512,128]{1,0:T(8,128)} %bitcast.21), channel_id=1, source_target_pairs={{0,1},{1,2},{2,3},{3,4},{4,5},{5,6},{6,7},{7,8},{8,9},{9,10},{10,1... | collective-permute-start | bytes 786440 | tf_op jit(solution)/shard_map/ppermute | solution.py:582
  2.0 4.6 %collective-permute-start.2 = (f32[512,128]{1,0:T(8,128)}, f32[512,128]{1,0:T(8,128)S(1)}, u32[]{:S(2)}, u32[]{:S(2)}) collective-permute-start(f32[512,128]{1,0:T(8,128)} %bitcast.22), channel_id=1, source_target_pairs={{0,15},{1,0},{2,1},{3,2},{4,3},{5,4},{6,5},{7,6},{8,7},{9,8},{10,9... | collective-permute-start | bytes 786440 | tf_op jit(solution)/shard_map/ppermute | solution.py:582
  6.6 5.3 %collective-permute-start.3 = (f32[3,1,512]{2,1,0:T(1,128)}, f32[3,1,512]{2,1,0:T(1,128)S(1)}, u32[]{:S(2)}, u32[]{:S(2)}) collective-permute-start(f32[3,1,512]{2,1,0:T(1,128)} %bitcast.13), channel_id=1, source_target_pairs={{0,15},{1,0},{2,1},{3,2},{4,3},{5,4},{6,5},{7,6},{8,7},{9,8},{10,9... | collective-permute-start | bytes 18440 | tf_op jit(solution)/shard_map/ppermute | solution.py:582
  11.9 5.1 %spread.1 = f32[3072,128]{1,0:T(8,128)} custom-call(f32[512,128]{1,0:T(8,128)} %bitcast.23, f32[3,1,512]{2,1,0:T(1,128)} %bitcast.14, f32[128,128]{1,0:T(8,128)} %refs_2_.2), custom_call_target="tpu_custom_call" | custom-call | flops 1200000000 | bytes 4194304 | tf_op jit(solution)/shard_map/spread/pallas_call | solution.py:527
  17.0 0.0 copy-start.13
  17.0 0.0 copy-start.10
  17.0 5.0 %all-to-all-start = ((f32[128,24,128]{2,1,0:T(8,128)}), f32[128,24,128]{2,1,0:T(8,128)S(1)}, u32[]{:S(2)}, u32[]{:S(2)}) async-start(f32[128,24,128]{2,1,0:T(8,128)} %bitcast.3), calls=%async_computation | async-start | bytes 3145728 | tf_op jit(solution)/shard_map/all_to_all | solution.py:610
  22.0 0.1 fusion
  23.5 0.5 pack.1.refs_4_
  24.0 0.0 collective-permute-start.4
  24.0 2.9 %collective-permute-start.5 = (f32[1584,128]{1,0:T(8,128)S(1)}, f32[1584,128]{1,0:T(8,128)}, u32[]{:S(2)}, u32[]{:S(2)}) collective-permute-start(f32[1584,128]{1,0:T(8,128)S(1)} %pack.1.refs_4_), channel_id=1, source_target_pairs={{0,112},{16,0},{32,16},{48,32},{64,48},{80,64},{96,80},{112,96},{1... | collective-permute-start | bytes 2433032 | tf_op jit(solution)/shard_map/ppermute | solution.py:582
  26.9 5.9 %short_range.2.refs_2_ = f32[512,128]{1,0:T(8,128)S(1)} custom-call(s32[4,36]{1,0:T(4,128)S(1)} %convert_element_type.3.refs_0_, f32[3,1,512]{2,1,0:T(1,128)S(1)} %bitcast.16, f32[512,128]{1,0:T(8,128)S(1)} %bitcast.25, f32[16,128]{1,0:T(8,128)S(1)} %copy-done.12, f32[1584,128]{1,0:T(8,128)S(1)} %pack.1.refs_4_), custom_call_target="tpu_custom_call" | custom-call | flops 12000000000 | bytes 4194304 | tf_op jit(solution)/shard_map/short_range/pallas_call | solution.py:527
  32.8 13.6 %all-to-all-done = f32[128,24,128]{2,1,0:T(8,128)S(1)} async-done(((f32[128,24,128]{2,1,0:T(8,128)}), f32[128,24,128]{2,1,0:T(8,128)S(1)}, u32[]{:S(2)}, u32[]{:S(2)}) %all-to-all-start) | async-done | bytes 1572896 | tf_op jit(solution)/shard_map/all_to_all | solution.py:610
  46.4 5.5 %filter.1 = f32[3072,128]{1,0:T(8,128)} custom-call(f32[1]{0:T(128)S(6)} %copy.17.refs_0_, f32[1]{0:T(128)S(6)} %copy.18.refs_1_, f32[3072,128]{1,0:T(8,128)S(1)} %bitcast.10, bf16[832,256]{1,0:T(8,128)(2,1)} %constant.4.clone.refs_3_), custom_call_target="tpu_custom_call" | custom-call | flops 2000000000 | bytes 4194304 | tf_op jit(solution)/shard_map/filter/pallas_call | solution.py:527
  52.0 0.0 copy-start.1
  52.0 0.0 copy-start.2
  52.0 0.0 copy-start.6
  52.1 5.0 %all-to-all-start.1 = ((f32[128,24,128]{2,1,0:T(8,128)}), f32[128,24,128]{2,1,0:T(8,128)S(1)}, u32[]{:S(2)}, u32[]{:S(2)}) async-start(f32[128,24,128]{2,1,0:T(8,128)} %bitcast.5), calls=%async_computation.1 | async-start | bytes 3145728 | tf_op jit(solution)/shard_map/all_to_all | solution.py:622
  57.1 0.6 prepare.1
  57.7 1.3 %copy-done.8 = bf16[1920,512]{1,0:T(8,128)(2,1)} copy-done((bf16[1920,512]{1,0:T(8,128)(2,1)}, bf16[1920,512]{1,0:T(8,128)(2,1)S(1)}, u32[]{:S(2)}) %copy-start.8) | copy-done | bytes 1966104
  59.0 0.6 copy-done.11
  59.6 9.1 %short_range.3.refs_0_ = f32[512,128]{1,0:T(8,128)S(1)} custom-call(s32[4,36]{1,0:T(4,128)S(1)} %convert_element_type.3.refs_0_, f32[3,1,512]{2,1,0:T(1,128)S(1)} %bitcast.18, f32[512,128]{1,0:T(8,128)S(1)} %short_range.2.refs_2_, f32[16,128]{1,0:T(8,128)S(1)} %copy-done.12, f32[1584,128]{1,0:T(8,128)} %collective-permute-done.4.refs_4_, ...), custom_call_target="tpu_custom_call" | custom-call | flops 12000000000 | bytes 4194304 | tf_op jit(solution)/shard_map/short_range/pallas_call | solution.py:527
  68.8 12.5 %all-to-all-done.1 = f32[128,24,128]{2,1,0:T(8,128)S(1)} async-done(((f32[128,24,128]{2,1,0:T(8,128)}), f32[128,24,128]{2,1,0:T(8,128)S(1)}, u32[]{:S(2)}, u32[]{:S(2)}) %all-to-all-start.1) | async-done | bytes 1572896 | tf_op jit(solution)/shard_map/all_to_all | solution.py:622
  81.3 6.6 %final.1 = f32[512,128]{1,0:T(8,128)} custom-call(f32[512,128]{1,0:T(8,128)S(1)} %short_range.3.refs_0_, f32[3072,128]{1,0:T(8,128)S(1)} %bitcast.11, bf16[1920,512]{1,0:T(8,128)(2,1)} %copy-done.8, f32[16,512]{1,0:T(8,128)} %copy-done.11), custom_call_target="tpu_custom_call" | custom-call | flops 2400000000 | bytes 4194304 | tf_op jit(solution)/shard_map/final/pallas_call | solution.py:527
  (29 shorter events, 0.1 us)
Async XLA Ops:
  0.0 23.5 %collective-permute-start = (f32[512,128]{1,0:T(8,128)}, f32[512,128]{1,0:T(8,128)S(1)}, u32[]{:S(2)}, u32[]{:S(2)}) collective-permute-start(f32[512,128]{1,0:T(8,128)} %bitcast.21), channel_id=1, source_target_pairs={{0,1},{1,2},{2,3},{3,4},{4,5},{5,6},{6,7},{7,8},{8,9},{9,10},{10,1... | collective-permute-start | bytes 786440 | tf_op jit(solution)/shard_map/ppermute | solution.py:582
  2.0 21.5 %collective-permute-start.2 = (f32[512,128]{1,0:T(8,128)}, f32[512,128]{1,0:T(8,128)S(1)}, u32[]{:S(2)}, u32[]{:S(2)}) collective-permute-start(f32[512,128]{1,0:T(8,128)} %bitcast.22), channel_id=1, source_target_pairs={{0,15},{1,0},{2,1},{3,2},{4,3},{5,4},{6,5},{7,6},{8,7},{9,8},{10,9... | collective-permute-start | bytes 786440 | tf_op jit(solution)/shard_map/ppermute | solution.py:582
  6.6 16.9 %collective-permute-start.1 = (f32[3,1,512]{2,1,0:T(1,128)}, f32[3,1,512]{2,1,0:T(1,128)S(1)}, u32[]{:S(2)}, u32[]{:S(2)}) collective-permute-start(f32[3,1,512]{2,1,0:T(1,128)} %bitcast.12), channel_id=1, source_target_pairs={{0,1},{1,2},{2,3},{3,4},{4,5},{5,6},{6,7},{7,8},{8,9},{9,10},{10,1... | collective-permute-start | bytes 18440 | tf_op jit(solution)/shard_map/ppermute | solution.py:582
  6.6 16.9 %collective-permute-start.3 = (f32[3,1,512]{2,1,0:T(1,128)}, f32[3,1,512]{2,1,0:T(1,128)S(1)}, u32[]{:S(2)}, u32[]{:S(2)}) collective-permute-start(f32[3,1,512]{2,1,0:T(1,128)} %bitcast.13), channel_id=1, source_target_pairs={{0,15},{1,0},{2,1},{3,2},{4,3},{5,4},{6,5},{7,6},{8,7},{9,8},{10,9... | collective-permute-start | bytes 18440 | tf_op jit(solution)/shard_map/ppermute | solution.py:582
  17.0 5.0 %copy-start.13 = (s32[1,1,4,16]{3,2,1,0:T(4,128)S(1)}, s32[1,1,4,16]{3,2,1,0:T(4,128)}, u32[]{:S(2)}) copy-start(s32[1,1,4,16]{3,2,1,0:T(4,128)} %param.18) | copy-start | bytes 772
  17.0 6.5 %copy-start.5 = (f32[1,1,3,512]{3,1,2,0:T(1,128)S(1)}, f32[1,1,3,512]{3,1,2,0:T(1,128)}, u32[]{:S(2)}) copy-start(f32[1,1,3,512]{3,1,2,0:T(1,128)} %param.17) | copy-start | bytes 18436
  17.0 6.5 %copy-start.9 = (f32[1,1,512,128]{3,2,1,0:T(8,128)S(1)}, f32[1,1,512,128]{3,2,1,0:T(8,128)}, u32[]{:S(2)}) copy-start(f32[1,1,512,128]{3,2,1,0:T(8,128)} %param.16) | copy-start | bytes 786436
  17.0 6.5 %copy-start.10 = (f32[128,128]{1,0:T(8,128)S(1)}, f32[128,128]{1,0:T(8,128)}, u32[]{:S(2)}) copy-start(f32[128,128]{1,0:T(8,128)} %refs_6_.2) | copy-start | bytes 196612
  17.0 29.4 %all-to-all-start = ((f32[128,24,128]{2,1,0:T(8,128)}), f32[128,24,128]{2,1,0:T(8,128)S(1)}, u32[]{:S(2)}, u32[]{:S(2)}) async-start(f32[128,24,128]{2,1,0:T(8,128)} %bitcast.3), calls=%async_computation | async-start | bytes 3145728 | tf_op jit(solution)/shard_map/all_to_all | solution.py:610
  23.4 3.5 %copy-start.12 = (f32[16,128]{1,0:T(8,128)S(1)}, f32[16,128]{1,0:T(8,128)}, u32[]{:S(2)}) copy-start(f32[16,128]{1,0:T(8,128)} %refs_3_.5) | copy-start | bytes 24580
  24.0 35.7 %collective-permute-start.4 = (f32[1584,128]{1,0:T(8,128)S(1)}, f32[1584,128]{1,0:T(8,128)}, u32[]{:S(2)}, u32[]{:S(2)}) collective-permute-start(f32[1584,128]{1,0:T(8,128)S(1)} %pack.1.refs_4_), channel_id=1, source_target_pairs={{0,16},{16,32},{32,48},{48,64},{64,80},{80,96},{96,112},{112,0},{1... | collective-permute-start | bytes 2433032 | tf_op jit(solution)/shard_map/ppermute | solution.py:582
  24.0 35.6 %collective-permute-start.5 = (f32[1584,128]{1,0:T(8,128)S(1)}, f32[1584,128]{1,0:T(8,128)}, u32[]{:S(2)}, u32[]{:S(2)}) collective-permute-start(f32[1584,128]{1,0:T(8,128)S(1)} %pack.1.refs_4_), channel_id=1, source_target_pairs={{0,112},{16,0},{32,16},{48,32},{64,48},{80,64},{96,80},{112,96},{1... | collective-permute-start | bytes 2433032 | tf_op jit(solution)/shard_map/ppermute | solution.py:582
  52.0 5.1 %copy-start = (f32[128,256]{1,0:T(8,128)S(1)}, f32[128,256]{1,0:T(8,128)}, u32[]{:S(2)}) copy-start(f32[128,256]{1,0:T(8,128)} %refs_2_.3) | copy-start | bytes 393220
  52.0 5.1 %copy-start.1 = (f32[256,128]{1,0:T(8,128)S(1)}, f32[256,128]{1,0:T(8,128)}, u32[]{:S(2)}) copy-start(f32[256,128]{1,0:T(8,128)} %refs_3_.6) | copy-start | bytes 393220
  52.0 5.1 %copy-start.2 = (f32[128,256]{1,0:T(8,128)S(1)}, f32[128,256]{1,0:T(8,128)}, u32[]{:S(2)}) copy-start(f32[128,256]{1,0:T(8,128)} %refs_6_.3) | copy-start | bytes 393220
  52.0 5.1 %copy-start.3 = (f32[256,128]{1,0:T(8,128)S(1)}, f32[256,128]{1,0:T(8,128)}, u32[]{:S(2)}) copy-start(f32[256,128]{1,0:T(8,128)} %refs_7_.1) | copy-start | bytes 393220
  52.0 5.1 %copy-start.4 = (f32[128,128]{1,0:T(8,128)S(1)}, f32[128,128]{1,0:T(8,128)}, u32[]{:S(2)}) copy-start(f32[128,128]{1,0:T(8,128)} %refs_4_.1) | copy-start | bytes 196612
  52.0 5.1 %copy-start.6 = (f32[128]{0:T(128)S(1)}, f32[128]{0:T(128)}, u32[]{:S(2)}) copy-start(f32[128]{0:T(128)} %param.24) | copy-start | bytes 1540
  52.0 5.1 %copy-start.7 = (f32[128]{0:T(128)S(1)}, f32[128]{0:T(128)}, u32[]{:S(2)}) copy-start(f32[128]{0:T(128)} %param.28) | copy-start | bytes 1540
  52.1 29.3 %all-to-all-start.1 = ((f32[128,24,128]{2,1,0:T(8,128)}), f32[128,24,128]{2,1,0:T(8,128)S(1)}, u32[]{:S(2)}, u32[]{:S(2)}) async-start(f32[128,24,128]{2,1,0:T(8,128)} %bitcast.5), calls=%async_computation.1 | async-start | bytes 3145728 | tf_op jit(solution)/shard_map/all_to_all | solution.py:622
  57.7 1.3 %copy-start.8 = (bf16[1920,512]{1,0:T(8,128)(2,1)}, bf16[1920,512]{1,0:T(8,128)(2,1)S(1)}, u32[]{:S(2)}) copy-start(bf16[1920,512]{1,0:T(8,128)(2,1)S(1)} %get-tuple-element.11.refs_2_) | copy-start | bytes 5898244
  59.0 0.6 copy-start.11

commit v2 on v1

--- a/solution.py
+++ b/solution.py
@@ -20,11 +20,13 @@
 BASES = 16
 ROWS = 24
 PACK = 528
+TURN = 40
 FAR = 1000.0
 CUTOFF = 0.05
 MID = 8
 LIMIT = 32 * 1024 * 1024
 SHORT_COST = 12_000_000_000
+PACK_COST = 50_000_000
 PREPARE_COST = 1_000
 
 
@@ -59,17 +61,14 @@
     return pltpu.roll(x, 64, x.ndim - 1)
 
 
-def pack_body(feat_a, pos_a, feat_b, pos_b, feat_c, pos_c, proj_ref, out_ref):
-    proj = proj_ref[...]
-    for k, (feat, pos_ref) in enumerate(((feat_a, pos_a), (feat_b, pos_b), (feat_c, pos_c))):
-        base = k * PACK
-        out_ref[base : base + ATOMS, :] = dot3(feat[...], proj)
-        for d in range(3):
-            pos = pos_ref[d]
-            for t in range(4):
-                row = base + ATOMS + 4 * d + t
-                out_ref[row : row + 1, :] = pos[:, t * LANES : (t + 1) * LANES]
-        out_ref[base + ATOMS + 12 : base + PACK, :] = jnp.zeros((PACK - ATOMS - 12, LANES), F32)
+def pack_body(feat_ref, pos_ref, proj_ref, out_ref):
+    for d in range(3):
+        pos = pos_ref[d]
+        for t in range(4):
+            row = ATOMS + 4 * d + t
+            out_ref[row : row + 1, :] = pos[:, t * LANES : (t + 1) * LANES]
+    out_ref[ATOMS + 12 : PACK, :] = jnp.zeros((PACK - ATOMS - 12, LANES), F32)
+    out_ref[0:ATOMS, :] = dot3(feat_ref[...], proj_ref[...])
 
 
 def hat(distance):
@@ -99,11 +98,12 @@
     return jnp.concatenate(planes_of(uy, uz, half, z, row < 64), axis=0)
 
 
-def spread_body(feat_ref, pos_ref, proj_ref, out_ref):
+def spread_body(feat_ref, pos_ref, proj_ref, value_ref, pack_ref, out_ref):
     pos = rows_of(pos_ref)
     wh, wl = split(planes_across(pos))
     ux = pos[0:1, :] * 8.0
     charges = dot3(feat_ref[...], proj_ref[...]).T
+    pack_body(feat_ref, pos_ref, value_ref, pack_ref)
     highs, lows = [], []
     for x in range(9):
         high, low = split(charges * hat(ux - float(x)))
@@ -111,7 +111,10 @@
         lows.append(low)
     high = jnp.concatenate(highs, axis=0)
     low = jnp.concatenate(lows, axis=0)
-    result = dot(high, wh) + (dot(low, wh) + dot(high, wl))
+    both = jnp.concatenate([wh[:, 256:320], wl[:, 256:320]], axis=1)
+    wide = dot(high, jnp.concatenate([wh[:, :256], wl[:, :256], both], axis=1))
+    last = wide[:, 512:]
+    result = jnp.concatenate([wide[:, :256] + wide[:, 256:512], last + half_turn(last)], axis=1) + dot(low, wh)
     piece = lambda x, k: result[x * LANES : (x + 1) * LANES, k * LANES : (k + 1) * LANES]
     edge = [half_turn(piece(8, 0)), piece(8, 0), half_turn(piece(8, 1)), piece(8, 1), half_turn(piece(8, 2))]
     below = lane_iota((1, LANES)) < 64
@@ -190,7 +193,7 @@
         edge_ref[h * devices : (h + 1) * devices, :] = pltpu.roll(both, 16, 0)
 
     first_row = lax.broadcasted_iota(jnp.int32, (8, 1), 0) == 0
-    x_forward = table_ref[0:64, 0:192]
+    stacks = []
     for s in range(0, 16, 2):
         parts = []
         for k in range(4):
@@ -206,9 +209,12 @@
                     tile = tile + jnp.where(low, in_ref[below : below + 8, :], 0.0)
                 tiles.append(tile)
             parts.append(jnp.concatenate(tiles, axis=0))
-        result = dot(x_forward, stack_rows(jnp.concatenate(parts, axis=1)))
+        stacks.append(stack_rows(jnp.concatenate(parts, axis=1)))
+    x_forward = table_ref[0:64, 0:192]
+    for s, stack in zip(range(0, 16, 2), stacks):
+        result = dot(x_forward, stack)
         for k in range(4):
-            turn_ref[pl.ds(2 * s + k, MESH, stride=32), :] = result[:, k * LANES : (k + 1) * LANES]
+            turn_ref[pl.ds(2 * s + k, MESH, stride=TURN), :] = result[:, k * LANES : (k + 1) * LANES]
 
     kappa = screen_ref[0]
     kappa_sq = kappa * kappa
@@ -226,7 +232,7 @@
         planes = []
         for p in range(start, start + group, 2):
             pairs = jnp.concatenate(
-                [turn_ref[(2 * p + k) * 32 : (2 * p + k + 1) * 32, :] for k in range(4)], axis=1
+                [turn_ref[(2 * p + k) * TURN : (2 * p + k) * TURN + 32, :] for k in range(4)], axis=1
             )
             result = dot(y_forward, stack_rows(pairs))
             for k in range(2):
@@ -250,13 +256,13 @@
                 p = start + g + k
                 a = result[:32, k * LANES : (k + 1) * LANES]
                 b = result[32:, k * LANES : (k + 1) * LANES]
-                turn_ref[2 * p * 32 : 2 * p * 32 + 32, :] = jnp.where(low, a, half_turn(b))
-                turn_ref[2 * p * 32 + 32 : 2 * p * 32 + 64, :] = jnp.where(low, half_turn(a), b)
+                turn_ref[2 * p * TURN : 2 * p * TURN + 32, :] = jnp.where(low, a, half_turn(b))
+                turn_ref[(2 * p + 1) * TURN : (2 * p + 1) * TURN + 32, :] = jnp.where(low, half_turn(a), b)
 
     x_back = table_ref[768:832, 0:192]
     for s in range(0, 16, 2):
         pair = jnp.concatenate(
-            [turn_ref[pl.ds(2 * s + k, MESH, stride=32), :] for k in range(4)], axis=1
+            [turn_ref[pl.ds(2 * s + k, MESH, stride=TURN), :] for k in range(4)], axis=1
         )
         result = dot(x_back, stack_rows(pair))
         for w in range(8):
@@ -431,17 +437,18 @@
 
 
 def final_body(msg_ref, in_ref, set_ref, hat_ref, out_ref):
-    up = set_ref[0:256, 0:384]
-    down = jnp.concatenate([set_ref[256:384, :], set_ref[384:512, 0:256]], axis=1)
-    mesh_out = []
+    mesh_out, stacks = [], []
     width = 12
     for r in range(0, ROWS, width):
         cells = jnp.concatenate(
             [in_ref[pl.ds(r + k, LANES, stride=ROWS), :] for k in range(width)], axis=1
         )
         inverse = lax.rsqrt(jnp.mean(cells * cells, axis=0, keepdims=True) + 1e-06)
-        hidden = silu(dot(up, stack_rows(cells * inverse)))
-        result = dot(down, stack_rows(hidden))
+        stacks.append(stack_rows(cells * inverse))
+    up = set_ref[0:256, 0:384]
+    down = jnp.concatenate([set_ref[256:384, :], set_ref[384:512, 0:256]], axis=1)
+    for stack in stacks:
+        result = dot(down, stack_rows(silu(dot(up, stack))))
         mesh_out += [result[:, k * LANES : (k + 1) * LANES] for k in range(width)]
     below = lane_iota((1, LANES)) < 64
     top = mesh_out[16:]
@@ -536,13 +543,10 @@
     )(*operands)
 
 
-def pack_call(*operands):
-    return call(pack_body, "pack", [(3 * PACK, LANES)], "vvvvvvv", [], 12_000_000_000, operands)[0]
-
-
-def spread_call(feat, pos, proj):
-    operands = [in_hbm(x) for x in (feat, pos, proj)]
-    return call(spread_body, "spread", [(LANES * ROWS, LANES)], "hhh", [], 1_200_000_000, operands)[0]
+def spread_call(*operands):
+    operands = [in_hbm(x) for x in operands]
+    shapes = [(PACK, LANES), (LANES * ROWS, LANES)]
+    return call(spread_body, "spread", shapes, "hhhh", [], 1_200_000_000, operands)
 
 
 def prepare_call(*operands):
@@ -551,7 +555,7 @@
 
 
 def filter_call(screening, smearing, received):
-    scratch = [pltpu.VMEM((MESH * 32, LANES), F32), pltpu.VMEM((256, LANES), F32)]
+    scratch = [pltpu.VMEM((MESH * TURN, LANES), F32), pltpu.VMEM((256, LANES), F32)]
     operands = (screening, smearing, received, in_hbm(jnp.asarray(filter_tables())))
     shapes = [(LANES * ROWS, LANES)]
     cuts = {3: (0, 64, 832)}
@@ -602,13 +606,11 @@
 ):
     feat, pos = features[0, 0], positions.reshape(3, 1, ATOMS)
     everyone = ("wide", "sixteen")
-    feat_below = passed_along(feat, "sixteen", 1)
-    feat_above = passed_along(feat, "sixteen", -1)
-    pos_below = passed_along(pos, "sixteen", 1)
-    pos_above = passed_along(pos, "sixteen", -1)
-    spread = spread_call(feat, pos, charge_proj)
+    packed, spread = spread_call(feat, pos, charge_proj, value_proj)
+    below = passed_along(packed, "sixteen", 1)
+    above = passed_along(packed, "sixteen", -1)
     received = lax.all_to_all(spread, everyone, split_axis=0, concat_axis=0, tiled=True)
-    near = pack_call(feat_below, pos_below, feat, pos, feat_above, pos_above, value_proj)
+    near = jnp.concatenate([below, packed, above], axis=0)
     left = passed_along(near, "wide", 1)
     right = passed_along(near, "wide", -1)
     codes = jnp.arange(36, dtype=jnp.int32)

time: 88.4 us -> 83.7 us (0.947)
  Pallas kernels: 33.3 us -> 29.4 us
  starting transfers between devices: 24.8 us -> 21.2 us
  waiting for transfers between devices: 26.2 us -> 29 us
    ppermute x6 -> x4, starting transfers between devices: 14.9 us -> 9.68 us  [passed_along(): lax.ppermute(array, axis, [(i, (i + by) % count) for i in range(count)])]
    pallas_call x7 -> x6, Pallas kernels: 33.3 us -> 29.4 us  [call(): pl.pallas_call(kernel, out_shape=[jax.ShapeDtypeStruct(x, F32) if isinsta...]
    all_to_all x1, waiting for transfers between devices: 12.5 us -> 14.5 us  [on_device(): lax.all_to_all(filtered, everyone, split_axis=0, concat_axis=0, tiled=True)]
    all_to_all x1, starting transfers between devices: 4.96 us -> 6.52 us  [on_device(): lax.all_to_all(spread, everyone, split_axis=0, concat_axis=0, tiled=True)]
  transfers between devices with their start and end apart: 8 -> 6, of which waited for: 2 -> 2; matrix products, arithmetic and copies ran while one was open for 0% -> 0% of each run, Pallas kernels for 30% -> 21%
where the time goes in v2:
time: 83.7 us; the launch traced here: 83.4 us
  Pallas kernels  29.4 us (35%)
  waiting for transfers between devices  29 us (35%)
  starting transfers between devices  21.2 us (25%)
  local copies, waits for them, and re-layouts  2.02 us (2%)
  between operations  1.72 us (2%)
    pallas_call x6, Pallas kernels, call(): pl.pallas_call(kernel, out_shape=[jax.ShapeDtypeStruct(x, F32) if isinsta...  29.4 us
    all_to_all x1, waiting for transfers between devices, on_device(): lax.all_to_all(spread, everyone, split_axis=0, concat_axis=0, tiled=True)  14.5 us
    all_to_all x1, waiting for transfers between devices, on_device(): lax.all_to_all(filtered, everyone, split_axis=0, concat_axis=0, tiled=True)  14.5 us
    ppermute x4, starting transfers between devices, passed_along(): lax.ppermute(array, axis, [(i, (i + by) % count) for i in range(count)])  9.68 us
    all_to_all x1, starting transfers between devices, on_device(): lax.all_to_all(spread, everyone, split_axis=0, concat_axis=0, tiled=True)  6.52 us
    all_to_all x1, starting transfers between devices, on_device(): lax.all_to_all(filtered, everyone, split_axis=0, concat_axis=0, tiled=True)  4.97 us
    unnamed x28, local copies, waits for them, and re-layouts  2 us
  transfers between devices with their start and end apart: 6, of which 2 were waited for; matrix products, arithmetic and copies ran while one was open for 0% of the time, Pallas kernels for 21%

profile of v2, /device:TPU:0, one launch (start us, length us, event | category | flops | bytes accessed | tf_op | source)
XLA Modules:
  0.0 83.4 jit_solution(16337301793717927811)
XLA Ops:
  0.0 5.0 %spread.1 = (f32[528,128]{1,0:T(8,128)S(1)}, f32[3072,128]{1,0:T(8,128)}) custom-call(f32[512,128]{1,0:T(8,128)} %bitcast.18, f32[3,1,512]{2,1,0:T(1,128)} %bitcast.12, f32[128,128]{1,0:T(8,128)} %refs_2_.2, f32[128,128]{1,0:T(8,128)} %refs_3_.5), custom_call_target="tpu_custom_call" | custom-call | flops 1200000000 | bytes 4194304 | tf_op jit(solution)/shard_map/spread/pallas_call | solution.py:534
  5.0 2.1 %collective-permute-start = (f32[528,128]{1,0:T(8,128)S(1)}, f32[528,128]{1,0:T(8,128)S(1)}, u32[]{:S(2)}, u32[]{:S(2)}) collective-permute-start(f32[528,128]{1,0:T(8,128)S(1)} %get-tuple-element.12), channel_id=1, source_target_pairs={{0,1},{1,2},{2,3},{3,4},{4,5},{5,6},{6,7},{7,8},{8,9},{9,10},{10,1... | collective-permute-start | bytes 811016 | tf_op jit(solution)/shard_map/ppermute | solution.py:586
  7.1 4.7 %collective-permute-start.1 = (f32[528,128]{1,0:T(8,128)S(1)}, f32[528,128]{1,0:T(8,128)S(1)}, u32[]{:S(2)}, u32[]{:S(2)}) collective-permute-start(f32[528,128]{1,0:T(8,128)S(1)} %get-tuple-element.12), channel_id=1, source_target_pairs={{0,15},{1,0},{2,1},{3,2},{4,3},{5,4},{6,5},{7,6},{8,7},{9,8},{10,9... | collective-permute-start | bytes 811016 | tf_op jit(solution)/shard_map/ppermute | solution.py:586
  11.7 6.5 %all-to-all-start = ((f32[128,24,128]{2,1,0:T(8,128)}), f32[128,24,128]{2,1,0:T(8,128)S(1)}, u32[]{:S(2)}, u32[]{:S(2)}) async-start(f32[128,24,128]{2,1,0:T(8,128)} %bitcast.3), calls=%async_computation | async-start | bytes 3145728 | tf_op jit(solution)/shard_map/all_to_all | solution.py:612
  18.3 0.0 copy-start.5
  18.3 0.0 copy-start.9
  18.3 0.0 copy-start.11
  18.3 0.1 fusion
  19.8 0.0 collective-permute-start.2
  19.8 2.9 %collective-permute-start.3 = (f32[1584,128]{1,0:T(8,128)S(1)}, f32[1584,128]{1,0:T(8,128)}, u32[]{:S(2)}, u32[]{:S(2)}) collective-permute-start(f32[1584,128]{1,0:T(8,128)S(1)} %constant_dynamic-update-slice_fusion.refs_4_), channel_id=1, source_target_pairs={{0,112},{16,0},{32,16},{48,32},{64,48},{80,64},{96,80},{112,96},{1... | collective-permute-start | bytes 2433032 | tf_op jit(solution)/shard_map/ppermute | solution.py:586
  22.8 5.4 %short_range.2.refs_2_ = f32[512,128]{1,0:T(8,128)S(1)} custom-call(s32[4,36]{1,0:T(4,128)S(1)} %convert_element_type.3.refs_0_, f32[3,1,512]{2,1,0:T(1,128)S(1)} %bitcast.13, f32[512,128]{1,0:T(8,128)S(1)} %bitcast.19, f32[16,128]{1,0:T(8,128)S(1)} %copy-done.11, f32[1584,128]{1,0:T(8,128)S(1)} %constant_dynamic-update-slice_fusion.refs_4_), custom_call_target="tpu_custom_call" | custom-call | flops 12000000000 | bytes 4194304 | tf_op jit(solution)/shard_map/short_range/pallas_call | solution.py:534
  28.2 14.5 %all-to-all-done = f32[128,24,128]{2,1,0:T(8,128)S(1)} async-done(((f32[128,24,128]{2,1,0:T(8,128)}), f32[128,24,128]{2,1,0:T(8,128)S(1)}, u32[]{:S(2)}, u32[]{:S(2)}) %all-to-all-start) | async-done | bytes 1572896 | tf_op jit(solution)/shard_map/all_to_all | solution.py:612
  42.7 4.7 %filter.1 = f32[3072,128]{1,0:T(8,128)} custom-call(f32[1]{0:T(128)S(6)} %copy.19.refs_0_, f32[1]{0:T(128)S(6)} %copy.20.refs_1_, f32[3072,128]{1,0:T(8,128)S(1)} %bitcast.10, bf16[832,256]{1,0:T(8,128)(2,1)} %constant.4.clone.refs_3_), custom_call_target="tpu_custom_call" | custom-call | flops 2000000000 | bytes 4194304 | tf_op jit(solution)/shard_map/filter/pallas_call | solution.py:534
  47.4 0.0 copy-start
  47.4 0.0 copy-start.1
  47.4 0.0 copy-start.3
  47.5 0.0 copy-start.4
  47.5 5.0 %all-to-all-start.1 = ((f32[128,24,128]{2,1,0:T(8,128)}), f32[128,24,128]{2,1,0:T(8,128)S(1)}, u32[]{:S(2)}, u32[]{:S(2)}) async-start(f32[128,24,128]{2,1,0:T(8,128)} %bitcast.5), calls=%async_computation.1 | async-start | bytes 3145728 | tf_op jit(solution)/shard_map/all_to_all | solution.py:624
  52.5 0.6 prepare.1
  53.2 1.3 %copy-done.8 = bf16[1920,512]{1,0:T(8,128)(2,1)} copy-done((bf16[1920,512]{1,0:T(8,128)(2,1)}, bf16[1920,512]{1,0:T(8,128)(2,1)S(1)}, u32[]{:S(2)}) %copy-start.8) | copy-done | bytes 1966104
  54.5 0.6 copy-done.10
  55.1 7.2 %short_range.3.refs_0_ = f32[512,128]{1,0:T(8,128)S(1)} custom-call(s32[4,36]{1,0:T(4,128)S(1)} %convert_element_type.3.refs_0_, f32[3,1,512]{2,1,0:T(1,128)S(1)} %bitcast.15, f32[512,128]{1,0:T(8,128)S(1)} %short_range.2.refs_2_, f32[16,128]{1,0:T(8,128)S(1)} %copy-done.11, f32[1584,128]{1,0:T(8,128)} %collective-permute-done.2.refs_4_, ...), custom_call_target="tpu_custom_call" | custom-call | flops 12000000000 | bytes 4194304 | tf_op jit(solution)/shard_map/short_range/pallas_call | solution.py:534
  62.3 14.5 %all-to-all-done.1 = f32[128,24,128]{2,1,0:T(8,128)S(1)} async-done(((f32[128,24,128]{2,1,0:T(8,128)}), f32[128,24,128]{2,1,0:T(8,128)S(1)}, u32[]{:S(2)}, u32[]{:S(2)}) %all-to-all-start.1) | async-done | bytes 1572896 | tf_op jit(solution)/shard_map/all_to_all | solution.py:624
  76.7 6.5 %final.1 = f32[512,128]{1,0:T(8,128)} custom-call(f32[512,128]{1,0:T(8,128)S(1)} %short_range.3.refs_0_, f32[3072,128]{1,0:T(8,128)S(1)} %bitcast.11, bf16[1920,512]{1,0:T(8,128)(2,1)} %copy-done.8, f32[16,512]{1,0:T(8,128)} %copy-done.10), custom_call_target="tpu_custom_call" | custom-call | flops 2400000000 | bytes 4194304 | tf_op jit(solution)/shard_map/final/pallas_call | solution.py:534
  (25 shorter events, 0.1 us)
Async XLA Ops:
  5.0 14.7 %collective-permute-start = (f32[528,128]{1,0:T(8,128)S(1)}, f32[528,128]{1,0:T(8,128)S(1)}, u32[]{:S(2)}, u32[]{:S(2)}) collective-permute-start(f32[528,128]{1,0:T(8,128)S(1)} %get-tuple-element.12), channel_id=1, source_target_pairs={{0,1},{1,2},{2,3},{3,4},{4,5},{5,6},{6,7},{7,8},{8,9},{9,10},{10,1... | collective-permute-start | bytes 811016 | tf_op jit(solution)/shard_map/ppermute | solution.py:586
  7.1 12.7 %collective-permute-start.1 = (f32[528,128]{1,0:T(8,128)S(1)}, f32[528,128]{1,0:T(8,128)S(1)}, u32[]{:S(2)}, u32[]{:S(2)}) collective-permute-start(f32[528,128]{1,0:T(8,128)S(1)} %get-tuple-element.12), channel_id=1, source_target_pairs={{0,15},{1,0},{2,1},{3,2},{4,3},{5,4},{6,5},{7,6},{8,7},{9,8},{10,9... | collective-permute-start | bytes 811016 | tf_op jit(solution)/shard_map/ppermute | solution.py:586
  11.7 6.6 %copy-start.12 = (s32[1,1,4,16]{3,2,1,0:T(4,128)S(1)}, s32[1,1,4,16]{3,2,1,0:T(4,128)}, u32[]{:S(2)}) copy-start(s32[1,1,4,16]{3,2,1,0:T(4,128)} %param.18) | copy-start | bytes 772
  11.7 31.0 %all-to-all-start = ((f32[128,24,128]{2,1,0:T(8,128)}), f32[128,24,128]{2,1,0:T(8,128)S(1)}, u32[]{:S(2)}, u32[]{:S(2)}) async-start(f32[128,24,128]{2,1,0:T(8,128)} %bitcast.3), calls=%async_computation | async-start | bytes 3145728 | tf_op jit(solution)/shard_map/all_to_all | solution.py:612
  18.3 4.5 %copy-start.5 = (f32[1,1,3,512]{3,1,2,0:T(1,128)S(1)}, f32[1,1,3,512]{3,1,2,0:T(1,128)}, u32[]{:S(2)}) copy-start(f32[1,1,3,512]{3,1,2,0:T(1,128)} %param.17) | copy-start | bytes 18436
  18.3 4.5 %copy-start.9 = (f32[1,1,512,128]{3,2,1,0:T(8,128)S(1)}, f32[1,1,512,128]{3,2,1,0:T(8,128)}, u32[]{:S(2)}) copy-start(f32[1,1,512,128]{3,2,1,0:T(8,128)} %param.16) | copy-start | bytes 786436
  18.3 4.5 %copy-start.11 = (f32[16,128]{1,0:T(8,128)S(1)}, f32[16,128]{1,0:T(8,128)}, u32[]{:S(2)}) copy-start(f32[16,128]{1,0:T(8,128)} %refs_3_.7) | copy-start | bytes 24580
  19.8 35.2 %collective-permute-start.2 = (f32[1584,128]{1,0:T(8,128)S(1)}, f32[1584,128]{1,0:T(8,128)}, u32[]{:S(2)}, u32[]{:S(2)}) collective-permute-start(f32[1584,128]{1,0:T(8,128)S(1)} %constant_dynamic-update-slice_fusion.refs_4_), channel_id=1, source_target_pairs={{0,16},{16,32},{32,48},{48,64},{64,80},{80,96},{96,112},{112,0},{1... | collective-permute-start | bytes 2433032 | tf_op jit(solution)/shard_map/ppermute | solution.py:586
  19.8 35.2 %collective-permute-start.3 = (f32[1584,128]{1,0:T(8,128)S(1)}, f32[1584,128]{1,0:T(8,128)}, u32[]{:S(2)}, u32[]{:S(2)}) collective-permute-start(f32[1584,128]{1,0:T(8,128)S(1)} %constant_dynamic-update-slice_fusion.refs_4_), channel_id=1, source_target_pairs={{0,112},{16,0},{32,16},{48,32},{64,48},{80,64},{96,80},{112,96},{1... | collective-permute-start | bytes 2433032 | tf_op jit(solution)/shard_map/ppermute | solution.py:586
  47.4 5.1 %copy-start = (f32[128,256]{1,0:T(8,128)S(1)}, f32[128,256]{1,0:T(8,128)}, u32[]{:S(2)}) copy-start(f32[128,256]{1,0:T(8,128)} %refs_2_.3) | copy-start | bytes 393220
  47.4 5.1 %copy-start.1 = (f32[256,128]{1,0:T(8,128)S(1)}, f32[256,128]{1,0:T(8,128)}, u32[]{:S(2)}) copy-start(f32[256,128]{1,0:T(8,128)} %refs_3_.8) | copy-start | bytes 393220
  47.4 5.1 %copy-start.2 = (f32[128,256]{1,0:T(8,128)S(1)}, f32[128,256]{1,0:T(8,128)}, u32[]{:S(2)}) copy-start(f32[128,256]{1,0:T(8,128)} %refs_6_.1) | copy-start | bytes 393220
  47.4 5.1 %copy-start.3 = (f32[256,128]{1,0:T(8,128)S(1)}, f32[256,128]{1,0:T(8,128)}, u32[]{:S(2)}) copy-start(f32[256,128]{1,0:T(8,128)} %refs_7_.1) | copy-start | bytes 393220
  47.5 5.1 %copy-start.4 = (f32[128,128]{1,0:T(8,128)S(1)}, f32[128,128]{1,0:T(8,128)}, u32[]{:S(2)}) copy-start(f32[128,128]{1,0:T(8,128)} %refs_4_.1) | copy-start | bytes 196612
  47.5 5.1 %copy-start.6 = (f32[128]{0:T(128)S(1)}, f32[128]{0:T(128)}, u32[]{:S(2)}) copy-start(f32[128]{0:T(128)} %param.24) | copy-start | bytes 1540
  47.5 5.1 %copy-start.7 = (f32[128]{0:T(128)S(1)}, f32[128]{0:T(128)}, u32[]{:S(2)}) copy-start(f32[128]{0:T(128)} %param.28) | copy-start | bytes 1540
  47.5 29.3 %all-to-all-start.1 = ((f32[128,24,128]{2,1,0:T(8,128)}), f32[128,24,128]{2,1,0:T(8,128)S(1)}, u32[]{:S(2)}, u32[]{:S(2)}) async-start(f32[128,24,128]{2,1,0:T(8,128)} %bitcast.5), calls=%async_computation.1 | async-start | bytes 3145728 | tf_op jit(solution)/shard_map/all_to_all | solution.py:624
  53.2 1.3 %copy-start.8 = (bf16[1920,512]{1,0:T(8,128)(2,1)}, bf16[1920,512]{1,0:T(8,128)(2,1)S(1)}, u32[]{:S(2)}) copy-start(bf16[1920,512]{1,0:T(8,128)(2,1)S(1)} %get-tuple-element.15.refs_2_) | copy-start | bytes 5898244
  54.4 0.6 copy-start.10

commit v3 on v2

--- a/solution.py
+++ b/solution.py
@@ -98,7 +98,7 @@
     return jnp.concatenate(planes_of(uy, uz, half, z, row < 64), axis=0)
 
 
-def spread_body(feat_ref, pos_ref, proj_ref, value_ref, pack_ref, out_ref):
+def spread_body(pos_ref, feat_ref, proj_ref, value_ref, pack_ref, out_ref):
     pos = rows_of(pos_ref)
     wh, wl = split(planes_across(pos))
     ux = pos[0:1, :] * 8.0
@@ -179,7 +179,7 @@
 
 
 def filter_body(
-    screen_ref, smear_ref, in_ref, table_ref, out_ref, turn_ref, edge_ref
+    screen_ref, smear_ref, in_ref, first_ref, table_ref, out_ref, turn_ref, edge_ref
 ):
     devices = 128
     low = lane_iota((1, LANES)) < 64
@@ -210,7 +210,7 @@
                 tiles.append(tile)
             parts.append(jnp.concatenate(tiles, axis=0))
         stacks.append(stack_rows(jnp.concatenate(parts, axis=1)))
-    x_forward = table_ref[0:64, 0:192]
+    x_forward = first_ref[:, 0:192]
     for s, stack in zip(range(0, 16, 2), stacks):
         result = dot(x_forward, stack)
         for k in range(4):
@@ -294,9 +294,13 @@
 
 
 def short_body(
-    blocks, units, live_ref, pos_ref, part_ref, mix_ref, *rest
+    blocks, units, packs, extra, live_ref, pos_ref, part_ref, mix_ref, *rest
 ):
-    *packs, out_ref, val_ref, win_ref, own_ref = rest
+    packs, rest = rest[:packs], rest[packs:]
+    *rest, val_ref, win_ref, own_ref = rest
+    given = len(extra.operands)
+    out_ref = rest[given]
+    extra.body(*rest[:given], *rest[given + 1 :])
     lane = lane_iota((1, LANES))
     filled = jnp.concatenate([rows_of(pos_ref), jnp.zeros((5, ATOMS), F32)], axis=0)
     columns = filled.T
@@ -411,19 +415,22 @@
     return jnp.concatenate(split(x), axis=1)
 
 
-def prepare_body(pos_ref, gain_ref, up_ref, down_ref, long_ref, again_ref, aup_ref, adown_ref, out_ref, hat_out):
-    out_ref[0:256, 0:384] = stack_lanes(up_ref[...].T * gain_ref[...])
-    down = stack_lanes(down_ref[...].T)
-    out_ref[256:384, :] = down[:, :512]
-    out_ref[384:512, 0:256] = down[:, 512:]
-    out_ref[1536:1664, :] = beside((aup_ref[...].T * again_ref[...]).T)
-    out_ref[1664:1920, 0:256] = beside(adown_ref[...])
-    out_ref[384:512, 256:512] = beside(long_ref[...])
+def mesh_weights_body(gain_ref, up_ref, down_ref, out_ref):
+    out_ref[:, 0:256] = beside(up_ref[...].T * gain_ref[...])
+    high, low = split(down_ref[...].T)
+    out_ref[0:128, 256:512] = high
+    out_ref[128:256, 256:512] = low
+
+
+def prepare_body(pos_ref, long_ref, again_ref, aup_ref, adown_ref, out_ref, hat_out):
+    out_ref[1024:1152, :] = beside((aup_ref[...].T * again_ref[...]).T)
+    out_ref[1152:1408, 0:256] = beside(adown_ref[...])
+    out_ref[1152:1280, 256:512] = beside(long_ref[...])
     pos = rows_of(pos_ref)
     high, low = split(planes_down(pos))
     main = 2 * LANES
     pieces = [high[:main], high[:main], low[:main], high[main : main + 64], high[main : main + 64], low[main:]]
-    out_ref[512:1536, :] = jnp.concatenate(pieces, axis=0)
+    out_ref[0:1024, :] = jnp.concatenate(pieces, axis=0)
     ux = pos[0:1, :] * 8.0
     hats = [hat(ux - float(x)) for x in range(9)] + [jnp.zeros((7, ATOMS), F32)]
     hat_out[...] = jnp.concatenate(hats, axis=0)
@@ -436,7 +443,7 @@
     return wide[:, :width] + (wide[:, width:] + dot(low, pair[:, :width]))
 
 
-def final_body(msg_ref, in_ref, set_ref, hat_ref, out_ref):
+def final_body(msg_ref, in_ref, mesh_ref, set_ref, hat_ref, out_ref):
     mesh_out, stacks = [], []
     width = 12
     for r in range(0, ROWS, width):
@@ -445,8 +452,9 @@
         )
         inverse = lax.rsqrt(jnp.mean(cells * cells, axis=0, keepdims=True) + 1e-06)
         stacks.append(stack_rows(cells * inverse))
-    up = set_ref[0:256, 0:384]
-    down = jnp.concatenate([set_ref[256:384, :], set_ref[384:512, 0:256]], axis=1)
+    first = mesh_ref[...]
+    up = jnp.concatenate([first[:, :256], first[:, :128]], axis=1)
+    down = jnp.concatenate([first[:128, 256:], first[128:, 256:], first[:128, 256:]], axis=1)
     for stack in stacks:
         result = dot(down, stack_rows(silu(dot(up, stack))))
         mesh_out += [result[:, k * LANES : (k + 1) * LANES] for k in range(width)]
@@ -461,15 +469,15 @@
         rounded = last.astype(BF).astype(F32)
         both = jnp.where(below, rounded, half_turn(last - rounded))
         stacks.append(jnp.concatenate([high, low, high, both.astype(BF), rounded.astype(BF)], axis=1))
-    found = dot(jnp.concatenate(stacks, axis=0), set_ref[512:1536, :])
+    found = dot(jnp.concatenate(stacks, axis=0), set_ref[0:1024, :])
     total = None
     for x in range(9):
         term = found[x * LANES : (x + 1) * LANES] * hat_ref[x : x + 1, :]
         total = term if total is None else total + term
-    summed = msg_ref[...] + dot_beside(total.T, set_ref[384:512, 256:512])
+    summed = msg_ref[...] + dot_beside(total.T, set_ref[1152:1280, 256:512])
     inverse = lax.rsqrt(jnp.mean(summed * summed, axis=1, keepdims=True) + 1e-06)
-    hidden = silu(dot_beside(summed * inverse, set_ref[1536:1664, :]))
-    out_ref[...] = summed + dot_beside(hidden, set_ref[1664:1920, 0:256])
+    hidden = silu(dot_beside(summed * inverse, set_ref[1024:1152, :]))
+    out_ref[...] = summed + dot_beside(hidden, set_ref[1152:1408, 0:256])
 
 
 def whole():
@@ -550,19 +558,32 @@
 
 
 def prepare_call(*operands):
-    shapes = [jax.ShapeDtypeStruct((1920, 512), BF), (16, ATOMS)]
-    return call(prepare_body, "prepare", shapes, "v" * 8, [], PREPARE_COST, operands)
-
-
-def filter_call(screening, smearing, received):
+    shapes = [jax.ShapeDtypeStruct((1408, 512), BF), (16, ATOMS)]
+    return call(prepare_body, "prepare", shapes, "v" * 5, [], PREPARE_COST, operands)
+
+
+def first_table_extra():
+    table = jnp.asarray(filter_tables()[:MESH])
+    return Extra(copy_body, [jax.ShapeDtypeStruct(table.shape, BF)], (table,))
+
+
+def copy_body(source_ref, target_ref):
+    target_ref[...] = source_ref[...]
+
+
+def filter_call(screening, smearing, received, first):
     scratch = [pltpu.VMEM((MESH * TURN, LANES), F32), pltpu.VMEM((256, LANES), F32)]
-    operands = (screening, smearing, received, in_hbm(jnp.asarray(filter_tables())))
+    operands = (screening, smearing, received, first, in_hbm(jnp.asarray(filter_tables())))
     shapes = [(LANES * ROWS, LANES)]
-    cuts = {3: (0, 64, 832)}
-    return call(filter_body, "filter", shapes, "ssvh", scratch, 2_000_000_000, operands, cuts)[0]
-
-
-def short_call(mesh, blocks, *operands):
+    return call(filter_body, "filter", shapes, "ssvvh", scratch, 2_000_000_000, operands)[0]
+
+
+class Extra:
+    def __init__(self, body, shapes, operands):
+        self.body, self.shapes, self.operands = body, shapes, operands
+
+
+def short_call(mesh, blocks, extra, live, pos, part, mix, *packs):
     with jax.sharding.use_abstract_mesh(mesh.abstract_mesh):
         units = [pltpu.ACC(i)((BASES // 2 * CHUNK, 2 * LANES), F32) for i in range(2)]
     scratch = [
@@ -570,15 +591,17 @@
         pltpu.VMEM((len(blocks), 2, 16, LANES), F32),
         pltpu.VMEM((3 * ATOMS, LANES), F32),
     ]
-    body = functools.partial(short_body, blocks, units)
+    body = functools.partial(short_body, blocks, units, len(packs), extra)
+    operands = (live, pos, part, mix, *packs, *extra.operands)
     places = "s" + "v" * (len(operands) - 1)
-    return call(body, "short_range", [(ATOMS, LANES)], places, scratch, SHORT_COST, operands)[0]
-
-
-def final_call(messages, returned, weights, hats):
-    operands = (messages, returned, in_hbm(weights), in_hbm(hats))
-    cuts = {2: (0, 512, 1536, 1920)}
-    return call(final_body, "final", [(ATOMS, LANES)], "vvhh", [], 2_400_000_000, operands, cuts)[0]
+    shapes = [(ATOMS, LANES)] + extra.shapes
+    return call(body, "short_range", shapes, places, scratch, SHORT_COST, operands)
+
+
+def final_call(messages, returned, mesh, weights, hats):
+    operands = (messages, returned, mesh, in_hbm(weights), in_hbm(hats))
+    cuts = {3: (0, 1024, 1408)}
+    return call(final_body, "final", [(ATOMS, LANES)], "vvvhh", [], 2_400_000_000, operands, cuts)[0]
 
 
 def passed_along(array, axis, by):
@@ -606,7 +629,7 @@
 ):
     feat, pos = features[0, 0], positions.reshape(3, 1, ATOMS)
     everyone = ("wide", "sixteen")
-    packed, spread = spread_call(feat, pos, charge_proj, value_proj)
+    packed, spread = spread_call(pos, feat, charge_proj, value_proj)
     below = passed_along(packed, "sixteen", 1)
     above = passed_along(packed, "sixteen", -1)
     received = lax.all_to_all(spread, everyone, split_axis=0, concat_axis=0, tiled=True)
@@ -615,15 +638,17 @@
     right = passed_along(near, "wide", -1)
     codes = jnp.arange(36, dtype=jnp.int32)
     live = jnp.any(tile_lists[0, 0][:, :, None] == codes, axis=1).astype(jnp.int32)
-    prepared = prepare_call(
-        pos, mesh_gain[None], mesh_up, mesh_down, long_proj, atom_gain[None], atom_up, atom_down
+    prepared = prepare_call(pos, long_proj, atom_gain[None], atom_up, atom_down)
+    part, table = short_call(mesh, (3, 4, 5), first_table_extra(), live, pos, feat, radial_mix, near)
+    received, part, table = lax.optimization_barrier((received, part, table))
+    filtered = filter_call(screening, smearing, received, table)
+    returned = lax.all_to_all(filtered, everyone, split_axis=0, concat_axis=0, tiled=True)
+    shape = jax.ShapeDtypeStruct((256, 512), BF)
+    weights = Extra(mesh_weights_body, [shape], (mesh_gain[None], mesh_up, mesh_down))
+    messages, mesh_weights = short_call(
+        mesh, (0, 1, 2, 6, 7, 8), weights, live, pos, part, radial_mix, left, right
     )
-    part = short_call(mesh, (3, 4, 5), live, pos, feat, radial_mix, near)
-    received, part = lax.optimization_barrier((received, part))
-    filtered = filter_call(screening, smearing, received)
-    returned = lax.all_to_all(filtered, everyone, split_axis=0, concat_axis=0, tiled=True)
-    messages = short_call(mesh, (0, 1, 2, 6, 7, 8), live, pos, part, radial_mix, left, right)
-    updated = final_call(messages, returned, *prepared)
+    updated = final_call(messages, returned, mesh_weights, *prepared)
     return updated[None, None]
 
 

time: 83.7 us -> 82.6 us (0.987)
  waiting for transfers between devices: 29 us -> 20.9 us
  Pallas kernels: 29.4 us -> 33.7 us
  local copies, waits for them, and re-layouts: 2.02 us -> 4.57 us
    all_to_all x1, waiting for transfers between devices: 14.5 us -> 8.14 us  [on_device(): lax.all_to_all(filtered, everyone, split_axis=0, concat_axis=0, tiled=True)]
    pallas_call x6, Pallas kernels: 29.4 us -> 33.7 us  [call(): pl.pallas_call(kernel, out_shape=[jax.ShapeDtypeStruct(x, F32) if isinsta...]
    unnamed x28 -> x34, local copies, waits for them, and re-layouts: 2 us -> 4.55 us
    all_to_all x1, waiting for transfers between devices: 14.5 us -> 12.7 us  [on_device(): lax.all_to_all(spread, everyone, split_axis=0, concat_axis=0, tiled=True)]
  transfers between devices with their start and end apart: 6 -> 6, of which waited for: 2 -> 2; matrix products, arithmetic and copies ran while one was open for 0% -> 0% of each run, Pallas kernels for 21% -> 28%
where the time goes in v3:
time: 82.6 us; the launch traced here: 82.2 us
  Pallas kernels  33.7 us (41%)
  starting transfers between devices  21.2 us (26%)
  waiting for transfers between devices  20.9 us (25%)
  local copies, waits for them, and re-layouts  4.57 us (6%)
  between operations  1.72 us (2%)
    pallas_call x6, Pallas kernels, call(): pl.pallas_call(kernel, out_shape=[jax.ShapeDtypeStruct(x, F32) if isinsta...  33.7 us
    all_to_all x1, waiting for transfers between devices, on_device(): lax.all_to_all(spread, everyone, split_axis=0, concat_axis=0, tiled=True)  12.7 us
    ppermute x4, starting transfers between devices, passed_along(): lax.ppermute(array, axis, [(i, (i + by) % count) for i in range(count)])  9.68 us
    all_to_all x1, waiting for transfers between devices, on_device(): lax.all_to_all(filtered, everyone, split_axis=0, concat_axis=0, tiled=True)  8.14 us
    all_to_all x1, starting transfers between devices, on_device(): lax.all_to_all(spread, everyone, split_axis=0, concat_axis=0, tiled=True)  6.52 us
    all_to_all x1, starting transfers between devices, on_device(): lax.all_to_all(filtered, everyone, split_axis=0, concat_axis=0, tiled=True)  4.97 us
    unnamed x34, local copies, waits for them, and re-layouts  4.55 us
  transfers between devices with their start and end apart: 6, of which 2 were waited for; matrix products, arithmetic and copies ran while one was open for 0% of the time, Pallas kernels for 28%

profile of v3, /device:TPU:0, one launch (start us, length us, event | category | flops | bytes accessed | tf_op | source)
XLA Modules:
  0.0 82.2 jit_solution(15997238172342087673)
XLA Ops:
  0.0 4.9 %spread.1 = (f32[528,128]{1,0:T(8,128)S(1)}, f32[3072,128]{1,0:T(8,128)}) custom-call(f32[3,1,512]{2,1,0:T(1,128)} %bitcast.12, f32[512,128]{1,0:T(8,128)} %bitcast.17, f32[128,128]{1,0:T(8,128)} %refs_2_.1, f32[128,128]{1,0:T(8,128)} %refs_3_.4), custom_call_target="tpu_custom_call" | custom-call | flops 1200000000 | bytes 4194304 | tf_op jit(solution)/shard_map/spread/pallas_call | solution.py:542
  4.9 2.1 %collective-permute-start = (f32[528,128]{1,0:T(8,128)S(1)}, f32[528,128]{1,0:T(8,128)S(1)}, u32[]{:S(2)}, u32[]{:S(2)}) collective-permute-start(f32[528,128]{1,0:T(8,128)S(1)} %get-tuple-element.17), channel_id=1, source_target_pairs={{0,1},{1,2},{2,3},{3,4},{4,5},{5,6},{6,7},{7,8},{8,9},{9,10},{10,1... | collective-permute-start | bytes 811016 | tf_op jit(solution)/shard_map/ppermute | solution.py:609
  7.0 4.7 %collective-permute-start.1 = (f32[528,128]{1,0:T(8,128)S(1)}, f32[528,128]{1,0:T(8,128)S(1)}, u32[]{:S(2)}, u32[]{:S(2)}) collective-permute-start(f32[528,128]{1,0:T(8,128)S(1)} %get-tuple-element.17), channel_id=1, source_target_pairs={{0,15},{1,0},{2,1},{3,2},{4,3},{5,4},{6,5},{7,6},{8,7},{9,8},{10,9... | collective-permute-start | bytes 811016 | tf_op jit(solution)/shard_map/ppermute | solution.py:609
  11.6 6.5 %all-to-all-start = ((f32[128,24,128]{2,1,0:T(8,128)}), f32[128,24,128]{2,1,0:T(8,128)S(1)}, u32[]{:S(2)}, u32[]{:S(2)}) async-start(f32[128,24,128]{2,1,0:T(8,128)} %bitcast.3), calls=%async_computation | async-start | bytes 3145728 | tf_op jit(solution)/shard_map/all_to_all | solution.py:635
  18.1 0.0 copy-start.6
  18.2 0.0 copy-start.10
  18.2 0.0 copy-start.12
  18.2 0.1 fusion
  19.7 0.0 collective-permute-start.2
  19.7 2.9 %collective-permute-start.3 = (f32[1584,128]{1,0:T(8,128)S(1)}, f32[1584,128]{1,0:T(8,128)}, u32[]{:S(2)}, u32[]{:S(2)}) collective-permute-start(f32[1584,128]{1,0:T(8,128)S(1)} %constant_dynamic-update-slice_fusion.refs_4_), channel_id=1, source_target_pairs={{0,112},{16,0},{32,16},{48,32},{64,48},{80,64},{96,80},{112,96},{1... | collective-permute-start | bytes 2433032 | tf_op jit(solution)/shard_map/ppermute | solution.py:609
  22.7 7.1 %short_range.2 = (f32[512,128]{1,0:T(8,128)S(1)}, bf16[64,256]{1,0:T(8,128)(2,1)S(1)}) custom-call(s32[4,36]{1,0:T(4,128)S(1)} %convert_element_type.3.refs_0_, f32[3,1,512]{2,1,0:T(1,128)S(1)} %bitcast.13, f32[512,128]{1,0:T(8,128)S(1)} %bitcast.18, f32[16,128]{1,0:T(8,128)S(1)} %copy-done.10, f32[1584,128]{1,0:T(8,128)S(1)} %constant_dynamic-update-slice_fusion.refs_4_, ...), custom_call_target="tpu_custom_call" | custom-call | flops 12000000000 | bytes 4194304 | tf_op jit(solution)/shard_map/short_range/pallas_call | solution.py:542
  29.8 12.7 %all-to-all-done = f32[128,24,128]{2,1,0:T(8,128)S(1)} async-done(((f32[128,24,128]{2,1,0:T(8,128)}), f32[128,24,128]{2,1,0:T(8,128)S(1)}, u32[]{:S(2)}, u32[]{:S(2)}) %all-to-all-start) | async-done | bytes 1572896 | tf_op jit(solution)/shard_map/all_to_all | solution.py:635
  42.6 4.5 %filter.1 = f32[3072,128]{1,0:T(8,128)} custom-call(f32[1]{0:T(128)S(6)} %copy.20.refs_0_, f32[1]{0:T(128)S(6)} %copy.21.refs_1_, f32[3072,128]{1,0:T(8,128)S(1)} %bitcast.10, bf16[64,256]{1,0:T(8,128)(2,1)S(1)} %get-tuple-element.23.refs_3_, bf16[832,256]{1,0:T(8,128)(2,1)} %constant.7.clone.refs_4_), custom_call_target="tpu_custom_call" | custom-call | flops 2000000000 | bytes 4194304 | tf_op jit(solution)/shard_map/filter/pallas_call | solution.py:542
  47.1 0.0 copy-start
  47.1 5.0 %all-to-all-start.1 = ((f32[128,24,128]{2,1,0:T(8,128)}), f32[128,24,128]{2,1,0:T(8,128)S(1)}, u32[]{:S(2)}, u32[]{:S(2)}) async-start(f32[128,24,128]{2,1,0:T(8,128)} %bitcast.6), calls=%async_computation.1 | async-start | bytes 3145728 | tf_op jit(solution)/shard_map/all_to_all | solution.py:645
  52.2 0.5 prepare.1
  52.7 1.1 %copy-done.5 = bf16[1408,512]{1,0:T(8,128)(2,1)} copy-done((bf16[1408,512]{1,0:T(8,128)(2,1)}, bf16[1408,512]{1,0:T(8,128)(2,1)S(1)}, u32[]{:S(2)}) %copy-start.5) | copy-done | bytes 1441816
  53.8 0.6 copy-done.9
  54.4 0.9 %copy-done.7 = f32[128,256]{1,0:T(8,128)S(1)} copy-done((f32[128,256]{1,0:T(8,128)S(1)}, f32[128,256]{1,0:T(8,128)}, u32[]{:S(2)}) %copy-start.7) | copy-done | bytes 131096
  55.3 0.9 %copy-done.8 = f32[256,128]{1,0:T(8,128)S(1)} copy-done((f32[256,128]{1,0:T(8,128)S(1)}, f32[256,128]{1,0:T(8,128)}, u32[]{:S(2)}) %copy-start.8) | copy-done | bytes 131096
  56.2 0.9 %copy-done.14 = f32[512,128]{1,0:T(8,128)S(1)} copy-done((f32[512,128]{1,0:T(8,128)S(1)}, f32[512,128]{1,0:T(8,128)}, u32[]{:S(2)}) %copy-start.14) | copy-done | bytes 262168
  57.2 11.1 %short_range.3 = (f32[512,128]{1,0:T(8,128)S(1)}, bf16[256,512]{1,0:T(8,128)(2,1)S(1)}) custom-call(s32[4,36]{1,0:T(4,128)S(1)} %convert_element_type.3.refs_0_, f32[3,1,512]{2,1,0:T(1,128)S(1)} %bitcast.15, f32[512,128]{1,0:T(8,128)S(1)} %copy-done.14, f32[16,128]{1,0:T(8,128)S(1)} %copy-done.10, f32[1584,128]{1,0:T(8,128)S(1)} %collective-permute-done.2.refs_4_, ...), custom_call_target="tpu_custom_call" | custom-call | flops 12000000000 | bytes 4194304 | tf_op jit(solution)/shard_map/short_range/pallas_call | solution.py:542
  68.3 8.1 %all-to-all-done.1 = f32[128,24,128]{2,1,0:T(8,128)S(1)} async-done(((f32[128,24,128]{2,1,0:T(8,128)}), f32[128,24,128]{2,1,0:T(8,128)S(1)}, u32[]{:S(2)}, u32[]{:S(2)}) %all-to-all-start.1) | async-done | bytes 1572896 | tf_op jit(solution)/shard_map/all_to_all | solution.py:645
  76.4 5.6 %final.1 = f32[512,128]{1,0:T(8,128)} custom-call(f32[512,128]{1,0:T(8,128)S(1)} %get-tuple-element.21.refs_0_, f32[3072,128]{1,0:T(8,128)S(1)} %bitcast.11, bf16[256,512]{1,0:T(8,128)(2,1)S(1)} %get-tuple-element.24.refs_2_, bf16[1408,512]{1,0:T(8,128)(2,1)} %copy-done.5, f32[16,512]{1,0:T(8,128)} %copy-done.9), custom_call_target="tpu_custom_call" | custom-call | flops 2400000000 | bytes 4194304 | tf_op jit(solution)/shard_map/final/pallas_call | solution.py:542
  (31 shorter events, 0.1 us)
Async XLA Ops:
  4.9 14.7 %collective-permute-start = (f32[528,128]{1,0:T(8,128)S(1)}, f32[528,128]{1,0:T(8,128)S(1)}, u32[]{:S(2)}, u32[]{:S(2)}) collective-permute-start(f32[528,128]{1,0:T(8,128)S(1)} %get-tuple-element.17), channel_id=1, source_target_pairs={{0,1},{1,2},{2,3},{3,4},{4,5},{5,6},{6,7},{7,8},{8,9},{9,10},{10,1... | collective-permute-start | bytes 811016 | tf_op jit(solution)/shard_map/ppermute | solution.py:609
  7.0 12.7 %collective-permute-start.1 = (f32[528,128]{1,0:T(8,128)S(1)}, f32[528,128]{1,0:T(8,128)S(1)}, u32[]{:S(2)}, u32[]{:S(2)}) collective-permute-start(f32[528,128]{1,0:T(8,128)S(1)} %get-tuple-element.17), channel_id=1, source_target_pairs={{0,15},{1,0},{2,1},{3,2},{4,3},{5,4},{6,5},{7,6},{8,7},{9,8},{10,9... | collective-permute-start | bytes 811016 | tf_op jit(solution)/shard_map/ppermute | solution.py:609
  11.6 6.6 %copy-start.15 = (s32[1,1,4,16]{3,2,1,0:T(4,128)S(1)}, s32[1,1,4,16]{3,2,1,0:T(4,128)}, u32[]{:S(2)}) copy-start(s32[1,1,4,16]{3,2,1,0:T(4,128)} %param.19) | copy-start | bytes 772
  11.6 31.0 %all-to-all-start = ((f32[128,24,128]{2,1,0:T(8,128)}), f32[128,24,128]{2,1,0:T(8,128)S(1)}, u32[]{:S(2)}, u32[]{:S(2)}) async-start(f32[128,24,128]{2,1,0:T(8,128)} %bitcast.3), calls=%async_computation | async-start | bytes 3145728 | tf_op jit(solution)/shard_map/all_to_all | solution.py:635
  18.1 4.5 %copy-start.3 = (f32[1,1,3,512]{3,1,2,0:T(1,128)S(1)}, f32[1,1,3,512]{3,1,2,0:T(1,128)}, u32[]{:S(2)}) copy-start(f32[1,1,3,512]{3,1,2,0:T(1,128)} %param.18) | copy-start | bytes 18436
  18.1 4.5 %copy-start.6 = (f32[1,1,512,128]{3,2,1,0:T(8,128)S(1)}, f32[1,1,512,128]{3,2,1,0:T(8,128)}, u32[]{:S(2)}) copy-start(f32[1,1,512,128]{3,2,1,0:T(8,128)} %param.17) | copy-start | bytes 786436
  18.2 4.5 %copy-start.10 = (f32[16,128]{1,0:T(8,128)S(1)}, f32[16,128]{1,0:T(8,128)}, u32[]{:S(2)}) copy-start(f32[16,128]{1,0:T(8,128)} %refs_3_.6) | copy-start | bytes 24580
  18.2 4.5 %copy-start.12 = (bf16[64,256]{1,0:T(8,128)(2,1)S(1)}, bf16[64,256]{1,0:T(8,128)(2,1)}, u32[]{:S(2)}) copy-start(bf16[64,256]{1,0:T(8,128)(2,1)} %constant.6.clone.refs_5_) | copy-start | bytes 98308
  19.7 34.7 %collective-permute-start.2 = (f32[1584,128]{1,0:T(8,128)S(1)}, f32[1584,128]{1,0:T(8,128)S(1)}, u32[]{:S(2)}, u32[]{:S(2)}) collective-permute-start(f32[1584,128]{1,0:T(8,128)S(1)} %constant_dynamic-update-slice_fusion.refs_4_), channel_id=1, source_target_pairs={{0,16},{16,32},{32,48},{48,64},{64,80},{80,96},{96,112},{112,0},{1... | collective-permute-start | bytes 2433032 | tf_op jit(solution)/shard_map/ppermute | solution.py:609
  19.7 34.7 %collective-permute-start.3 = (f32[1584,128]{1,0:T(8,128)S(1)}, f32[1584,128]{1,0:T(8,128)}, u32[]{:S(2)}, u32[]{:S(2)}) collective-permute-start(f32[1584,128]{1,0:T(8,128)S(1)} %constant_dynamic-update-slice_fusion.refs_4_), channel_id=1, source_target_pairs={{0,112},{16,0},{32,16},{48,32},{64,48},{80,64},{96,80},{112,96},{1... | collective-permute-start | bytes 2433032 | tf_op jit(solution)/shard_map/ppermute | solution.py:609
  29.8 17.2 %copy-start.13 = (f32[512,128]{1,0:T(8,128)}, f32[512,128]{1,0:T(8,128)S(1)}, u32[]{:S(2)}) copy-start(f32[512,128]{1,0:T(8,128)S(1)} %get-tuple-element.20.refs_2_) | copy-start | bytes 786436
  47.1 5.0 %copy-start = (f32[128,256]{1,0:T(8,128)S(1)}, f32[128,256]{1,0:T(8,128)}, u32[]{:S(2)}) copy-start(f32[128,256]{1,0:T(8,128)} %refs_3_.7) | copy-start | bytes 393220
  47.1 5.0 %copy-start.1 = (f32[256,128]{1,0:T(8,128)S(1)}, f32[256,128]{1,0:T(8,128)}, u32[]{:S(2)}) copy-start(f32[256,128]{1,0:T(8,128)} %refs_4_.2) | copy-start | bytes 393220
  47.1 5.0 %copy-start.2 = (f32[128,128]{1,0:T(8,128)S(1)}, f32[128,128]{1,0:T(8,128)}, u32[]{:S(2)}) copy-start(f32[128,128]{1,0:T(8,128)} %refs_1_.2) | copy-start | bytes 196612
  47.1 5.0 %copy-start.4 = (f32[128]{0:T(128)S(1)}, f32[128]{0:T(128)}, u32[]{:S(2)}) copy-start(f32[128]{0:T(128)} %param.29) | copy-start | bytes 1540
  47.1 7.3 %copy-start.11 = (f32[128]{0:T(128)S(1)}, f32[128]{0:T(128)}, u32[]{:S(2)}) copy-start(f32[128]{0:T(128)} %param.25) | copy-start | bytes 1540
  47.1 29.3 %all-to-all-start.1 = ((f32[128,24,128]{2,1,0:T(8,128)}), f32[128,24,128]{2,1,0:T(8,128)S(1)}, u32[]{:S(2)}, u32[]{:S(2)}) async-start(f32[128,24,128]{2,1,0:T(8,128)} %bitcast.6), calls=%async_computation.1 | async-start | bytes 3145728 | tf_op jit(solution)/shard_map/all_to_all | solution.py:645
  52.7 1.1 %copy-start.5 = (bf16[1408,512]{1,0:T(8,128)(2,1)}, bf16[1408,512]{1,0:T(8,128)(2,1)S(1)}, u32[]{:S(2)}) copy-start(bf16[1408,512]{1,0:T(8,128)(2,1)S(1)} %get-tuple-element.25.refs_3_) | copy-start | bytes 4325380
  53.8 0.6 copy-start.9
  54.4 0.9 %copy-start.7 = (f32[128,256]{1,0:T(8,128)S(1)}, f32[128,256]{1,0:T(8,128)}, u32[]{:S(2)}) copy-start(f32[128,256]{1,0:T(8,128)} %refs_7_.1) | copy-start | bytes 393220
  55.3 0.9 %copy-start.8 = (f32[256,128]{1,0:T(8,128)S(1)}, f32[256,128]{1,0:T(8,128)}, u32[]{:S(2)}) copy-start(f32[256,128]{1,0:T(8,128)} %refs_8_.1) | copy-start | bytes 393220
  56.2 0.9 %copy-start.14 = (f32[512,128]{1,0:T(8,128)S(1)}, f32[512,128]{1,0:T(8,128)}, u32[]{:S(2)}) copy-start(f32[512,128]{1,0:T(8,128)} %copy-done.13) | copy-start | bytes 786436

commit v4 on v3

--- a/solution.py
+++ b/solution.py
@@ -25,7 +25,7 @@
 CUTOFF = 0.05
 MID = 8
 LIMIT = 32 * 1024 * 1024
-SHORT_COST = 12_000_000_000
+SHORT_COST = 24_000_000_000
 PACK_COST = 50_000_000
 PREPARE_COST = 1_000
 

time: 82.6 us -> 82.6 us (level)
  waiting for transfers between devices: 20.9 us -> 27 us
  Pallas kernels: 33.7 us -> 29.9 us
  local copies, waits for them, and re-layouts: 4.57 us -> 2.37 us
    all_to_all x1, waiting for transfers between devices: 8.14 us -> 15.2 us  [on_device(): lax.all_to_all(filtered, everyone, split_axis=0, concat_axis=0, tiled=True)]
    pallas_call x6, Pallas kernels: 33.7 us -> 29.9 us  [call(): pl.pallas_call(kernel, out_shape=[jax.ShapeDtypeStruct(x, F32) if isinsta...]
    unnamed x34, local copies, waits for them, and re-layouts: 4.55 us -> 2.35 us
    all_to_all x1, waiting for transfers between devices: 12.7 us -> 11.7 us  [on_device(): lax.all_to_all(spread, everyone, split_axis=0, concat_axis=0, tiled=True)]
  transfers between devices with their start and end apart: 6 -> 6, of which waited for: 2 -> 2; matrix products, arithmetic and copies ran while one was open for 0% -> 0% of each run, Pallas kernels for 28% -> 23%
where the time goes in v4:
time: 82.6 us; the launch traced here: 82.2 us
  Pallas kernels  29.9 us (36%)
  waiting for transfers between devices  27 us (33%)
  starting transfers between devices  21.2 us (26%)
  local copies, waits for them, and re-layouts  2.37 us (3%)
  between operations  1.75 us (2%)
    pallas_call x6, Pallas kernels, call(): pl.pallas_call(kernel, out_shape=[jax.ShapeDtypeStruct(x, F32) if isinsta...  29.9 us
    all_to_all x1, waiting for transfers between devices, on_device(): lax.all_to_all(filtered, everyone, split_axis=0, concat_axis=0, tiled=True)  15.2 us
    all_to_all x1, waiting for transfers between devices, on_device(): lax.all_to_all(spread, everyone, split_axis=0, concat_axis=0, tiled=True)  11.7 us
    ppermute x4, starting transfers between devices, passed_along(): lax.ppermute(array, axis, [(i, (i + by) % count) for i in range(count)])  9.68 us
    all_to_all x1, starting transfers between devices, on_device(): lax.all_to_all(spread, everyone, split_axis=0, concat_axis=0, tiled=True)  6.52 us
    all_to_all x1, starting transfers between devices, on_device(): lax.all_to_all(filtered, everyone, split_axis=0, concat_axis=0, tiled=True)  4.97 us
    unnamed x34, local copies, waits for them, and re-layouts  2.35 us
  transfers between devices with their start and end apart: 6, of which 2 were waited for; matrix products, arithmetic and copies ran while one was open for 0% of the time, Pallas kernels for 23%

profile of v4, /device:TPU:0, one launch (start us, length us, event | category | flops | bytes accessed | tf_op | source)
XLA Modules:
  0.0 82.2 jit_solution(2173273337036054775)
XLA Ops:
  0.0 4.8 %spread.1 = (f32[528,128]{1,0:T(8,128)S(1)}, f32[3072,128]{1,0:T(8,128)}) custom-call(f32[3,1,512]{2,1,0:T(1,128)} %bitcast.12, f32[512,128]{1,0:T(8,128)} %bitcast.17, f32[128,128]{1,0:T(8,128)} %refs_2_.1, f32[128,128]{1,0:T(8,128)} %refs_3_.4), custom_call_target="tpu_custom_call" | custom-call | flops 1200000000 | bytes 4194304 | tf_op jit(solution)/shard_map/spread/pallas_call | solution.py:542
  4.8 2.1 %collective-permute-start = (f32[528,128]{1,0:T(8,128)S(1)}, f32[528,128]{1,0:T(8,128)S(1)}, u32[]{:S(2)}, u32[]{:S(2)}) collective-permute-start(f32[528,128]{1,0:T(8,128)S(1)} %get-tuple-element.17), channel_id=1, source_target_pairs={{0,1},{1,2},{2,3},{3,4},{4,5},{5,6},{6,7},{7,8},{8,9},{9,10},{10,1... | collective-permute-start | bytes 811016 | tf_op jit(solution)/shard_map/ppermute | solution.py:609
  6.9 4.7 %collective-permute-start.1 = (f32[528,128]{1,0:T(8,128)S(1)}, f32[528,128]{1,0:T(8,128)S(1)}, u32[]{:S(2)}, u32[]{:S(2)}) collective-permute-start(f32[528,128]{1,0:T(8,128)S(1)} %get-tuple-element.17), channel_id=1, source_target_pairs={{0,15},{1,0},{2,1},{3,2},{4,3},{5,4},{6,5},{7,6},{8,7},{9,8},{10,9... | collective-permute-start | bytes 811016 | tf_op jit(solution)/shard_map/ppermute | solution.py:609
  11.6 0.0 copy-start.4
  11.6 6.5 %all-to-all-start = ((f32[128,24,128]{2,1,0:T(8,128)}), f32[128,24,128]{2,1,0:T(8,128)S(1)}, u32[]{:S(2)}, u32[]{:S(2)}) async-start(f32[128,24,128]{2,1,0:T(8,128)} %bitcast.3), calls=%async_computation | async-start | bytes 3145728 | tf_op jit(solution)/shard_map/all_to_all | solution.py:635
  18.1 0.0 copy-start.6
  18.2 0.0 copy-start.12
  18.2 0.1 fusion
  18.3 0.5 prepare.1
  18.9 0.6 copy-done.9
  20.9 0.0 collective-permute-start.2
  20.9 2.9 %collective-permute-start.3 = (f32[1584,128]{1,0:T(8,128)S(1)}, f32[1584,128]{1,0:T(8,128)}, u32[]{:S(2)}, u32[]{:S(2)}) collective-permute-start(f32[1584,128]{1,0:T(8,128)S(1)} %constant_dynamic-update-slice_fusion.refs_4_), channel_id=1, source_target_pairs={{0,112},{16,0},{32,16},{48,32},{64,48},{80,64},{96,80},{112,96},{1... | collective-permute-start | bytes 2433032 | tf_op jit(solution)/shard_map/ppermute | solution.py:609
  23.9 6.3 %short_range.2 = (f32[512,128]{1,0:T(8,128)S(1)}, bf16[64,256]{1,0:T(8,128)(2,1)S(1)}) custom-call(s32[4,36]{1,0:T(4,128)S(1)} %convert_element_type.3.refs_0_, f32[3,1,512]{2,1,0:T(1,128)S(1)} %bitcast.14, f32[512,128]{1,0:T(8,128)S(1)} %bitcast.18, f32[16,128]{1,0:T(8,128)S(1)} %copy-done.10, f32[1584,128]{1,0:T(8,128)S(1)} %constant_dynamic-update-slice_fusion.refs_4_, ...), custom_call_target="tpu_custom_call" | custom-call | flops 24000000000 | bytes 4194304 | tf_op jit(solution)/shard_map/short_range/pallas_call | solution.py:542
  30.1 0.0 copy-start.13
  30.2 0.7 copy-done.13
  30.8 11.7 %all-to-all-done = f32[128,24,128]{2,1,0:T(8,128)S(1)} async-done(((f32[128,24,128]{2,1,0:T(8,128)}), f32[128,24,128]{2,1,0:T(8,128)S(1)}, u32[]{:S(2)}, u32[]{:S(2)}) %all-to-all-start) | async-done | bytes 1572896 | tf_op jit(solution)/shard_map/all_to_all | solution.py:635
  42.6 4.4 %filter.1 = f32[3072,128]{1,0:T(8,128)} custom-call(f32[1]{0:T(128)S(6)} %copy.20.refs_0_, f32[1]{0:T(128)S(6)} %copy.21.refs_1_, f32[3072,128]{1,0:T(8,128)S(1)} %bitcast.10, bf16[64,256]{1,0:T(8,128)(2,1)S(1)} %get-tuple-element.23.refs_3_, bf16[832,256]{1,0:T(8,128)(2,1)} %constant.7.clone.refs_4_), custom_call_target="tpu_custom_call" | custom-call | flops 2000000000 | bytes 4194304 | tf_op jit(solution)/shard_map/filter/pallas_call | solution.py:542
  47.0 0.0 copy-start.8
  47.1 0.0 copy-start.11
  47.1 5.0 %all-to-all-start.1 = ((f32[128,24,128]{2,1,0:T(8,128)}), f32[128,24,128]{2,1,0:T(8,128)S(1)}, u32[]{:S(2)}, u32[]{:S(2)}) async-start(f32[128,24,128]{2,1,0:T(8,128)} %bitcast.6), calls=%async_computation.1 | async-start | bytes 3145728 | tf_op jit(solution)/shard_map/all_to_all | solution.py:645
  52.1 0.9 %copy-done.14 = f32[512,128]{1,0:T(8,128)S(1)} copy-done((f32[512,128]{1,0:T(8,128)S(1)}, f32[512,128]{1,0:T(8,128)}, u32[]{:S(2)}) %copy-start.14) | copy-done | bytes 262168
  53.0 8.1 %short_range.3 = (f32[512,128]{1,0:T(8,128)S(1)}, bf16[256,512]{1,0:T(8,128)(2,1)S(1)}) custom-call(s32[4,36]{1,0:T(4,128)S(1)} %convert_element_type.3.refs_0_, f32[3,1,512]{2,1,0:T(1,128)S(1)} %bitcast.15, f32[512,128]{1,0:T(8,128)S(1)} %copy-done.14, f32[16,128]{1,0:T(8,128)S(1)} %copy-done.10, f32[1584,128]{1,0:T(8,128)S(1)} %collective-permute-done.2.refs_4_, ...), custom_call_target="tpu_custom_call" | custom-call | flops 24000000000 | bytes 4194304 | tf_op jit(solution)/shard_map/short_range/pallas_call | solution.py:542
  61.1 15.2 %all-to-all-done.1 = f32[128,24,128]{2,1,0:T(8,128)S(1)} async-done(((f32[128,24,128]{2,1,0:T(8,128)}), f32[128,24,128]{2,1,0:T(8,128)S(1)}, u32[]{:S(2)}, u32[]{:S(2)}) %all-to-all-start.1) | async-done | bytes 1572896 | tf_op jit(solution)/shard_map/all_to_all | solution.py:645
  76.3 5.7 %final.1 = f32[512,128]{1,0:T(8,128)} custom-call(f32[512,128]{1,0:T(8,128)S(1)} %get-tuple-element.21.refs_0_, f32[3072,128]{1,0:T(8,128)S(1)} %bitcast.11, bf16[256,512]{1,0:T(8,128)(2,1)S(1)} %get-tuple-element.24.refs_2_, bf16[1408,512]{1,0:T(8,128)(2,1)} %copy-done.5, f32[16,512]{1,0:T(8,128)} %copy-done.9), custom_call_target="tpu_custom_call" | custom-call | flops 2400000000 | bytes 4194304 | tf_op jit(solution)/shard_map/final/pallas_call | solution.py:542
  (31 shorter events, 0.1 us)
Async XLA Ops:
  4.8 15.9 %collective-permute-start = (f32[528,128]{1,0:T(8,128)S(1)}, f32[528,128]{1,0:T(8,128)S(1)}, u32[]{:S(2)}, u32[]{:S(2)}) collective-permute-start(f32[528,128]{1,0:T(8,128)S(1)} %get-tuple-element.17), channel_id=1, source_target_pairs={{0,1},{1,2},{2,3},{3,4},{4,5},{5,6},{6,7},{7,8},{8,9},{9,10},{10,1... | collective-permute-start | bytes 811016 | tf_op jit(solution)/shard_map/ppermute | solution.py:609
  6.9 13.9 %collective-permute-start.1 = (f32[528,128]{1,0:T(8,128)S(1)}, f32[528,128]{1,0:T(8,128)S(1)}, u32[]{:S(2)}, u32[]{:S(2)}) collective-permute-start(f32[528,128]{1,0:T(8,128)S(1)} %get-tuple-element.17), channel_id=1, source_target_pairs={{0,15},{1,0},{2,1},{3,2},{4,3},{5,4},{6,5},{7,6},{8,7},{9,8},{10,9... | collective-permute-start | bytes 811016 | tf_op jit(solution)/shard_map/ppermute | solution.py:609
  11.6 6.6 %copy-start.15 = (s32[1,1,4,16]{3,2,1,0:T(4,128)S(1)}, s32[1,1,4,16]{3,2,1,0:T(4,128)}, u32[]{:S(2)}) copy-start(s32[1,1,4,16]{3,2,1,0:T(4,128)} %param.19) | copy-start | bytes 772
  11.6 6.7 %copy-start = (f32[128,256]{1,0:T(8,128)S(1)}, f32[128,256]{1,0:T(8,128)}, u32[]{:S(2)}) copy-start(f32[128,256]{1,0:T(8,128)} %refs_3_.7) | copy-start | bytes 393220
  11.6 6.7 %copy-start.1 = (f32[256,128]{1,0:T(8,128)S(1)}, f32[256,128]{1,0:T(8,128)}, u32[]{:S(2)}) copy-start(f32[256,128]{1,0:T(8,128)} %refs_4_.2) | copy-start | bytes 393220
  11.6 6.7 %copy-start.2 = (f32[128,128]{1,0:T(8,128)S(1)}, f32[128,128]{1,0:T(8,128)}, u32[]{:S(2)}) copy-start(f32[128,128]{1,0:T(8,128)} %refs_1_.2) | copy-start | bytes 196612
  11.6 6.7 %copy-start.3 = (f32[1,1,3,512]{3,1,2,0:T(1,128)S(1)}, f32[1,1,3,512]{3,1,2,0:T(1,128)}, u32[]{:S(2)}) copy-start(f32[1,1,3,512]{3,1,2,0:T(1,128)} %param.18) | copy-start | bytes 18436
  11.6 6.7 %copy-start.4 = (f32[128]{0:T(128)S(1)}, f32[128]{0:T(128)}, u32[]{:S(2)}) copy-start(f32[128]{0:T(128)} %param.29) | copy-start | bytes 1540
  11.6 31.0 %all-to-all-start = ((f32[128,24,128]{2,1,0:T(8,128)}), f32[128,24,128]{2,1,0:T(8,128)S(1)}, u32[]{:S(2)}, u32[]{:S(2)}) async-start(f32[128,24,128]{2,1,0:T(8,128)} %bitcast.3), calls=%async_computation | async-start | bytes 3145728 | tf_op jit(solution)/shard_map/all_to_all | solution.py:635
  18.1 5.7 %copy-start.6 = (f32[1,1,512,128]{3,2,1,0:T(8,128)S(1)}, f32[1,1,512,128]{3,2,1,0:T(8,128)}, u32[]{:S(2)}) copy-start(f32[1,1,512,128]{3,2,1,0:T(8,128)} %param.17) | copy-start | bytes 786436
  18.1 5.7 %copy-start.10 = (f32[16,128]{1,0:T(8,128)S(1)}, f32[16,128]{1,0:T(8,128)}, u32[]{:S(2)}) copy-start(f32[16,128]{1,0:T(8,128)} %refs_3_.6) | copy-start | bytes 24580
  18.2 5.7 %copy-start.12 = (bf16[64,256]{1,0:T(8,128)(2,1)S(1)}, bf16[64,256]{1,0:T(8,128)(2,1)}, u32[]{:S(2)}) copy-start(bf16[64,256]{1,0:T(8,128)(2,1)} %constant.6.clone.refs_5_) | copy-start | bytes 98308
  18.9 0.6 copy-start.9
  19.5 1.4 %copy-start.5 = (bf16[1408,512]{1,0:T(8,128)(2,1)}, bf16[1408,512]{1,0:T(8,128)(2,1)S(1)}, u32[]{:S(2)}) copy-start(bf16[1408,512]{1,0:T(8,128)(2,1)S(1)} %get-tuple-element.25.refs_3_) | copy-start | bytes 4325380
  20.9 31.2 %collective-permute-start.2 = (f32[1584,128]{1,0:T(8,128)S(1)}, f32[1584,128]{1,0:T(8,128)S(1)}, u32[]{:S(2)}, u32[]{:S(2)}) collective-permute-start(f32[1584,128]{1,0:T(8,128)S(1)} %constant_dynamic-update-slice_fusion.refs_4_), channel_id=1, source_target_pairs={{0,16},{16,32},{32,48},{48,64},{64,80},{80,96},{96,112},{112,0},{1... | collective-permute-start | bytes 2433032 | tf_op jit(solution)/shard_map/ppermute | solution.py:609
  20.9 31.1 %collective-permute-start.3 = (f32[1584,128]{1,0:T(8,128)S(1)}, f32[1584,128]{1,0:T(8,128)}, u32[]{:S(2)}, u32[]{:S(2)}) collective-permute-start(f32[1584,128]{1,0:T(8,128)S(1)} %constant_dynamic-update-slice_fusion.refs_4_), channel_id=1, source_target_pairs={{0,112},{16,0},{32,16},{48,32},{64,48},{80,64},{96,80},{112,96},{1... | collective-permute-start | bytes 2433032 | tf_op jit(solution)/shard_map/ppermute | solution.py:609
  30.1 0.7 copy-start.13
  47.0 5.0 %copy-start.7 = (f32[128,256]{1,0:T(8,128)S(1)}, f32[128,256]{1,0:T(8,128)}, u32[]{:S(2)}) copy-start(f32[128,256]{1,0:T(8,128)} %refs_7_.1) | copy-start | bytes 393220
  47.0 5.0 %copy-start.8 = (f32[256,128]{1,0:T(8,128)S(1)}, f32[256,128]{1,0:T(8,128)}, u32[]{:S(2)}) copy-start(f32[256,128]{1,0:T(8,128)} %refs_8_.1) | copy-start | bytes 393220
  47.1 5.0 %copy-start.11 = (f32[128]{0:T(128)S(1)}, f32[128]{0:T(128)}, u32[]{:S(2)}) copy-start(f32[128]{0:T(128)} %param.25) | copy-start | bytes 1540
  47.1 29.3 %all-to-all-start.1 = ((f32[128,24,128]{2,1,0:T(8,128)}), f32[128,24,128]{2,1,0:T(8,128)S(1)}, u32[]{:S(2)}, u32[]{:S(2)}) async-start(f32[128,24,128]{2,1,0:T(8,128)} %bitcast.6), calls=%async_computation.1 | async-start | bytes 3145728 | tf_op jit(solution)/shard_map/all_to_all | solution.py:645
  52.1 1.0 %copy-start.14 = (f32[512,128]{1,0:T(8,128)S(1)}, f32[512,128]{1,0:T(8,128)}, u32[]{:S(2)}) copy-start(f32[512,128]{1,0:T(8,128)} %copy-done.13) | copy-start | bytes 786436
